TPU v7x, 256 devices: a whole 4x4x8 slice. The times are simulated.
256 devices in a mesh: tm: 64 (over z, y, core), tensor: 4 (over x).
Axes of the slice: x: 4, y: 4, z: 8, core: 2. Of those that a mesh axis runs over, the one named last changes fastest.
Arguments:
- frames_in: bfloat16 [64, 1024, 768], P('tm'), may hold values from -16 to 16
- norm_gain: float32 [768], replicated, may hold values from 0.1 to 1.9
- w_qkv: bfloat16 [768, 3, 768], P(None, None, 'tensor'), may hold values from -0.21650635 to 0.21650635
- w_out: bfloat16 [768, 768], P('tensor'), may hold values from -0.21875 to 0.21875
- keep_runs: int32 [64, 16, 2], replicated, may hold values from 0 to 1023, as said below
- out_cotangent: bfloat16 [64, 1024, 768], P('tm'), may hold values from -16 to 16
Outputs:
- block_out: bfloat16 [64, 1024, 768], P('tm', None, 'tensor')
- grad_in: bfloat16 [64, 1024, 768], P('tm', None, 'tensor')
- grad_qkv: bfloat16 [768, 3, 768], P('tm', None, 'tensor')
- grad_proj: bfloat16 [768, 768], P('tensor', 'tm')
- grad_gain: float32 [768], P('tensor')
Inputs may be any that keep to these rules, and one draw needn't show every extreme that they name: keep_runs[t, r] = (first, length) is the r-th run of kept positions of frame t; the 16 runs of a frame are disjoint, in rising order, and lie within the frame's 1024 positions.
All inputs are finite; a program needn't handle non-finite values.
Results may differ from a plain program's by a relative error of at most 0.034.
Values may be sent and summed in bfloat16 or wider, within the bound.
A program may use at most 128 MiB of HBM per device.

v0:
```python
import jax
import jax.numpy as jnp
from jax import lax
from jax.sharding import PartitionSpec as P

D = 768
H = 12


epsilon = 1e-05


def kept_table(keep_runs, first_place, place_count):
    places = first_place + jnp.arange(place_count, dtype=jnp.int32)
    starts = keep_runs[:, :, 0:1]
    lengths = keep_runs[:, :, 1:2]
    inside = (places[None, None, :] >= starts) & (places[None, None, :] < starts + lengths)
    return jnp.sum(inside.astype(jnp.int32), axis=1)


def normalize(frames_in):
    frames_float = frames_in.astype(jnp.float32)
    centre = jnp.mean(frames_float, axis=-1, keepdims=True)
    shifted = frames_float - centre
    spread = jnp.mean(shifted * shifted, axis=-1, keepdims=True)
    inverse_spread = lax.rsqrt(spread + epsilon)
    return (frames_float, shifted * inverse_spread, inverse_spread)


def attend(packed, kept_mask):
    frames, places, row_width = packed.shape
    head_width = D // H
    pieces = packed.reshape(frames, places, 3, row_width // (3 * head_width), head_width)
    scores = jnp.einsum(
        "tphd,uphd->phtu", pieces[:, :, 0], pieces[:, :, 1], preferred_element_type=jnp.float32
    )
    scores = scores * head_width ** (-0.5)
    allowed = jnp.transpose(kept_mask)[:, None, None, :] > 0
    scores = jnp.where(allowed, scores, -1000000000.0)
    row_max = jnp.max(scores, axis=-1, keepdims=True)
    exponent = jnp.exp(scores - row_max)
    weights = (exponent / jnp.sum(exponent, axis=-1, keepdims=True)).astype(jnp.bfloat16)
    mixed_rows = jnp.einsum(
        "phtu,uphd->tphd", weights, pieces[:, :, 2], preferred_element_type=jnp.float32
    )
    mixed_rows = jnp.where(kept_mask[:, :, None, None] > 0, mixed_rows, 0.0)
    return mixed_rows.astype(jnp.bfloat16).reshape(frames, places, row_width // 3)


def project(rows_in, weight):
    leading = rows_in.shape[:-1]
    flat = jnp.dot(
        rows_in.reshape(-1, rows_in.shape[-1]), weight, preferred_element_type=jnp.float32
    )
    return flat.astype(jnp.bfloat16).reshape(leading + (weight.shape[1],))


def contract_rows(left, right):
    return lax.dot_general(
        left.reshape(-1, left.shape[-1]),
        right.reshape(-1, right.shape[-1]),
        (((0,), (0,)), ((), ())),
        preferred_element_type=jnp.float32,
    )


def back_project(cotangent, weight):
    leading = cotangent.shape[:-1]
    flat = lax.dot_general(
        cotangent.reshape(-1, cotangent.shape[-1]),
        weight,
        (((1,), (1,)), ((), ())),
        preferred_element_type=jnp.float32,
    )
    return flat.reshape(leading + (weight.shape[0],))


def body(frames_in, norm_gain, w_qkv, w_out, keep_runs, out_cotangent):
    frames_here, place_total, row_width = frames_in.shape
    places_here = place_total // lax.axis_size("tm")
    width_share = row_width // lax.axis_size("tensor")
    share_start = lax.axis_index("tensor") * width_share
    channels = w_qkv.shape[2]
    w_flat = w_qkv.reshape(row_width, 3 * channels)
    kept_mask = kept_table(keep_runs, lax.axis_index("tm") * places_here, places_here)
    frames_float, standard, inverse_spread = normalize(frames_in)
    normed = (standard * norm_gain).astype(jnp.bfloat16)
    packed = project(normed, w_flat)
    packed_places = lax.all_to_all(packed, "tm", split_axis=1, concat_axis=0, tiled=True)

    def attend_here(packed_arg):
        return attend(packed_arg, kept_mask)

    mixed_places, attend_back = jax.vjp(attend_here, packed_places)
    mixed_frames = lax.all_to_all(mixed_places, "tm", split_axis=0, concat_axis=1, tiled=True)
    branch = jnp.dot(mixed_frames.reshape(-1, channels), w_out, preferred_element_type=jnp.float32)
    branch = branch.reshape(frames_here, place_total, row_width)
    branch_share = lax.psum_scatter(
        branch.astype(jnp.bfloat16), "tensor", scatter_dimension=2, tiled=True
    ).astype(jnp.float32)
    residual_share = lax.dynamic_slice_in_dim(frames_float, share_start, width_share, 2)
    block_out = (residual_share + branch_share).astype(jnp.bfloat16)
    proj_part = contract_rows(mixed_frames, out_cotangent)
    grad_proj = lax.psum_scatter(proj_part, "tm", scatter_dimension=1, tiled=True).astype(
        jnp.bfloat16
    )
    mixed_cot = back_project(out_cotangent, w_out).astype(jnp.bfloat16)
    mixed_cot_places = lax.all_to_all(mixed_cot, "tm", split_axis=1, concat_axis=0, tiled=True)
    packed_cot_places = attend_back(mixed_cot_places)[0]
    gain_share = lax.dynamic_slice_in_dim(norm_gain, share_start, width_share, 0)
    standard_share = lax.dynamic_slice_in_dim(standard, share_start, width_share, 2)
    packed_cot = lax.all_to_all(packed_cot_places, "tm", split_axis=0, concat_axis=1, tiled=True)
    qkv_part = contract_rows(normed, packed_cot)
    normed_part = back_project(packed_cot, w_flat)
    whole_cot = lax.psum(normed_part.astype(jnp.bfloat16), "tensor").astype(jnp.float32)
    whole_cot = lax.optimization_barrier(whole_cot.astype(jnp.bfloat16)).astype(jnp.float32)
    scaled_whole = whole_cot * norm_gain
    mean_plain = jnp.mean(scaled_whole, axis=-1, keepdims=True)
    mean_cross = jnp.mean(scaled_whole * standard, axis=-1, keepdims=True)
    cot_share = lax.dynamic_slice_in_dim(whole_cot, share_start, width_share, 2)
    scaled_share = cot_share * gain_share
    through = inverse_spread * (scaled_share - mean_plain - standard_share * mean_cross)
    gain_part = jnp.sum(cot_share * standard_share, axis=(0, 1))
    cot_share_out = lax.dynamic_slice_in_dim(out_cotangent, share_start, width_share, 2).astype(
        jnp.float32
    )
    grad_in = (cot_share_out + through).astype(jnp.bfloat16)
    grad_qkv = lax.psum_scatter(
        qkv_part.reshape(row_width, 3, channels), "tm", scatter_dimension=0, tiled=True
    ).astype(jnp.bfloat16)
    grad_gain = lax.psum(gain_part, "tm")
    return (block_out, grad_in, grad_qkv, grad_proj, grad_gain)


def solution(mesh):
    in_specs = (
        P("tm", None, None),
        P(),
        P(None, None, "tensor"),
        P("tensor", None),
        P(),
        P("tm", None, None),
    )
    out_specs = (
        P("tm", None, "tensor"),
        P("tm", None, "tensor"),
        P("tm", None, "tensor"),
        P("tensor", "tm"),
        P("tensor"),
    )
    return jax.shard_map(body, mesh=mesh, in_specs=in_specs, out_specs=out_specs, check_vma=False)
```

profile of v0, /device:TPU:2, one launch (start us, length us, event | category | flops | bytes accessed | tf_op | source)
XLA Modules:
  0.0 647.4 jit_solution(4025349044222602225)
XLA Ops:
  10.7 4.9 reduce.9
  18.1 12.3 %all-to-all-start.2 = ((bf16[64,2,1536]{2,1,0:T(2,128)(2,1)}), bf16[64,2,1536]{2,1,0:T(2,128)(2,1)S(1)}, u32[]{:S(2)}, u32[]{:S(2)}) async-start(bf16[64,2,1536]{2,1,0:T(2,128)(2,1)} %reshape.164), calls=%async_computation.2 | async-start | bytes 786432 | tf_op jit(solution)/shard_map/all_to_all | solution.py:108
  33.6 6.2 copy.70
  39.8 11.0 %reduce.8 = bf16[1024,576]{1,0:T(8,128)(2,1)} reduce(bf16[1024,1,576]{2,1,0:T(2,128)(2,1)} %bitcast.116, bf16[]{:T(256)} %broadcast.99), dimensions={1}, to_apply=%bitcast.89.reduce_sub_computation | reduce | bytes 2359298
  50.8 4.3 reshape.162
  55.1 10.7 %all-to-all-start = ((bf16[64,2,4608]{2,1,0:T(2,128)(2,1)}), bf16[64,2,4608]{2,1,0:T(2,128)(2,1)}, u32[]{:S(2)}, u32[]{:S(2)}) async-start(bf16[64,2,4608]{2,1,0:T(2,128)(2,1)} %reshape.162), calls=%async_computation | async-start | bytes 2359296 | tf_op jit(solution)/shard_map/all_to_all | solution.py:89
  66.0 3.8 reshape.165
  69.8 3.8 convert_reduce_fusion.2
  77.7 19.6 %all-to-all-done = bf16[64,2,4608]{2,1,0:T(2,128)(2,1)} async-done(((bf16[64,2,4608]{2,1,0:T(2,128)(2,1)}), bf16[64,2,4608]{2,1,0:T(2,128)(2,1)}, u32[]{:S(2)}, u32[]{:S(2)}) %all-to-all-start) | async-done | bytes 1179680 | tf_op jit(solution)/shard_map/all_to_all | solution.py:89
  97.3 9.1 %reshape.163 = bf16[1024,1,576]{2,1,0:T(2,128)(2,1)} reshape(bf16[64,2,4608]{2,1,0:T(2,128)(2,1)} %all-to-all-done) | data formatting | bytes 2359296
  106.4 10.3 %bitcast_reduce_fusion = bf16[1024,576]{1,0:T(8,128)(2,1)} fusion(bf16[1024,1,576]{2,1,0:T(2,128)(2,1)} %reshape.163), kind=kLoop, calls=%fused_computation.97 | loop fusion | bytes 2359296 | tf_op jit(solution)/shard_map/all_to_all | solution.py:89
  116.8 6.7 %reshape.145 = bf16[64,16,3,3,64]{4,3,2,1,0:T(4,128)(2,1)} reshape(bf16[1024,576]{1,0:T(8,128)(2,1)} %bitcast_reduce_fusion) | data formatting | bytes 2359296 | tf_op jit(solution)/shard_map/jvp()/reshape | solution.py:33
  123.5 5.2 fusion.69
  130.5 3.3 fusion.73
  144.0 4.5 copy.84
  148.5 40.0 %all_to_all.16 = bf16[64,16,576]{2,1,0:T(8,128)(2,1)S(1)} all-to-all(bf16[64,16,576]{2,1,0:T(8,128)(2,1)} %copy.84), channel_id=1, replica_groups=mesh['tm'=64,'tensor'=4] {'tm'}, dimensions={0} | all-to-all | bytes 2359296 | tf_op jit(solution)/shard_map/all_to_all | solution.py:112
  192.5 2.7 fusion.15
  197.1 22.9 %all_to_all.17 = bf16[64,16,192]{2,1,0:T(8,128)(2,1)S(1)} all-to-all(bf16[64,16,192]{2,1,0:T(8,128)(2,1)S(1)} %copy.75), channel_id=1, replica_groups=mesh['tm'=64,'tensor'=4] {'tm'}, dimensions={0} | all-to-all | bytes 786432 | tf_op jit(solution)/shard_map/all_to_all | solution.py:95
  219.9 2.7 fusion.21
  222.6 8.4 %copy.98 = bf16[1,1024,768]{1,0,2:T(2,128)(2,1)} copy(bf16[1,1024,768]{2,1,0:T(8,128)(2,1)} %fusion.21) | data formatting | bytes 3145728
  231.0 3.7 copy.117
  234.8 3.0 fusion.11
  237.8 57.0 %fusion = f32[192,16]{0,1:T(8,128)S(1)} fusion(f32[192,768]{0,1:T(8,128)} %fusion.11), kind=kCustom, calls=%all-reduce-scatter | all-reduce-scatter fusion | flops 196609 | bytes 603136
  298.3 3.0 collective-permute-start.1
  301.3 4.9 collective-permute-start.10
  306.2 6.9 %collective-permute-start.11 = (bf16[192,16]{0,1:T(8,128)(2,1)S(1)}, bf16[192,16]{0,1:T(8,128)(2,1)S(1)}, u32[]{:S(2)}, u32[]{:S(2)}) collective-permute-start(bf16[192,16]{0,1:T(8,128)(2,1)S(1)} %convert.31), channel_id=1, source_target_pairs={{0,48},{4,52},{8,56},{12,60},{16,64},{20,68},{24,72},{28,76},{32,8... | collective-permute-start | bytes 18440
  315.2 3.5 collective-permute-start.13
  322.2 3.8 collective-permute-start.3
  326.0 2.8 collective-permute-start.4
  328.8 4.4 collective-permute-start.5
  349.2 4.5 fusion.5
  359.1 273.6 %all-reduce.11 = (bf16[768,3,192]{2,0,1:T(8,128)(2,1)}, f32[192]{0:T(256)}) all-reduce(f32[768,3,192]{2,0,1:T(8,128)} %fusion.5, f32[192]{0:T(256)S(1)} %get-tuple-element.31), channel_id=3, replica_groups=mesh['tm'=64,'tensor'=4] {'tm'}, use_global_device_ids=true, to_apply=%region_12.13.clone | all-reduce | flops 442560 | bytes 2655744
  (107 shorter events, 67.6 us)
Async XLA Ops:
  7.2 24.1 %copy-start = (bf16[768,3,192]{0,2,1:T(8,128)(2,1)S(1)}, bf16[768,3,192]{0,2,1:T(8,128)(2,1)}, u32[]{:S(2)}) copy-start(bf16[768,3,192]{0,2,1:T(8,128)(2,1)} %param.8) | copy-start | bytes 2654212
  10.7 19.6 %copy-start.1 = (bf16[1,1024,768]{2,1,0:T(8,128)(2,1)S(1)}, bf16[1,1024,768]{2,1,0:T(8,128)(2,1)}, u32[]{:S(2)}) copy-start(bf16[1,1024,768]{2,1,0:T(8,128)(2,1)} %param.6) | copy-start | bytes 4718596
  18.1 37.0 %all-to-all-start.2 = ((bf16[64,2,1536]{2,1,0:T(2,128)(2,1)}), bf16[64,2,1536]{2,1,0:T(2,128)(2,1)S(1)}, u32[]{:S(2)}, u32[]{:S(2)}) async-start(bf16[64,2,1536]{2,1,0:T(2,128)(2,1)} %reshape.164), calls=%async_computation.2 | async-start | bytes 786432 | tf_op jit(solution)/shard_map/all_to_all | solution.py:108
  55.1 10.7 %copy-start.10 = (s32[64,16,2]{0,2,1:T(2,128)S(1)}, s32[64,16,2]{0,2,1:T(2,128)}, u32[]{:S(2)}) copy-start(s32[64,16,2]{0,2,1:T(2,128)} %param.10) | copy-start | bytes 24580
  55.1 10.9 %copy-start.7 = (bf16[64,2,1536]{2,1,0:T(2,128)(2,1)}, bf16[64,2,1536]{2,1,0:T(2,128)(2,1)S(1)}, u32[]{:S(2)}) copy-start(bf16[64,2,1536]{2,1,0:T(2,128)(2,1)S(1)} %all-to-all-done.2) | copy-start | bytes 1179652
  55.1 42.2 %all-to-all-start = ((bf16[64,2,4608]{2,1,0:T(2,128)(2,1)}), bf16[64,2,4608]{2,1,0:T(2,128)(2,1)}, u32[]{:S(2)}, u32[]{:S(2)}) async-start(bf16[64,2,4608]{2,1,0:T(2,128)(2,1)} %reshape.162), calls=%async_computation | async-start | bytes 2359296 | tf_op jit(solution)/shard_map/all_to_all | solution.py:89
  65.7 287.9 %all-reduce.10.cloned.1.call-start = ((), (), s32[]{:S(2)}) async-start(), calls=%async_computation.5 | async-start | bytes 3145728 | tf_op jit(solution)/shard_map/psum | solution.py:115
  133.8 7.0 %copy-start.2 = (f32[16,3,64,64]{2,3,1,0:T(8,128)}, f32[16,3,64,64]{2,3,1,0:T(8,128)S(1)}, u32[]{:S(2)}) copy-start(f32[16,3,64,64]{2,3,1,0:T(8,128)S(1)} %get-tuple-element.58) | copy-start | bytes 2359300
  133.9 1.7 copy-start.5
  133.9 1.9 copy-start.6
  136.5 1.2 copy-start.9
  137.8 1.6 copy-start.8
  188.6 1.1 copy-start.4
  192.2 442.9 %reduce-scatter.7.cloned.1.call-start = ((), (), s32[]{:S(2)}) async-start(), calls=%async_computation.6 | async-start | bytes 1966080
  294.8 18.3 %collective-permute-start.15 = (bf16[192,12]{0,1:T(8,128)(2,1)S(1)}, bf16[192,12]{0,1:T(8,128)(2,1)S(1)}, u32[]{:S(2)}, u32[]{:S(2)}) collective-permute-start(bf16[192,12]{0,1:T(8,128)(2,1)S(1)} %slice.23), channel_id=1, source_target_pairs={{0,64},{4,68},{8,72},{12,76},{16,80},{20,84},{24,88},{28,92},{32,9... | collective-permute-start | bytes 13832
  297.0 18.1 %collective-permute-start = (bf16[192,16]{0,1:T(8,128)(2,1)S(1)}, bf16[192,16]{0,1:T(8,128)(2,1)S(1)}, u32[]{:S(2)}, u32[]{:S(2)}) collective-permute-start(bf16[192,16]{0,1:T(8,128)(2,1)S(1)} %convert.31), channel_id=1, source_target_pairs={{0,4},{4,8},{8,12},{12,16},{16,20},{20,24},{24,28},{28,32},{32,36}... | collective-permute-start | bytes 18440
  298.3 20.4 %collective-permute-start.1 = (bf16[192,16]{0,1:T(8,128)(2,1)S(1)}, bf16[192,16]{0,1:T(8,128)(2,1)S(1)}, u32[]{:S(2)}, u32[]{:S(2)}) collective-permute-start(bf16[192,16]{0,1:T(8,128)(2,1)S(1)} %convert.31), channel_id=1, source_target_pairs={{0,8},{4,12},{8,16},{12,20},{16,24},{20,28},{24,32},{28,36},{32,40... | collective-permute-start | bytes 18440
  301.3 18.8 %collective-permute-start.10 = (bf16[192,16]{0,1:T(8,128)(2,1)S(1)}, bf16[192,16]{0,1:T(8,128)(2,1)S(1)}, u32[]{:S(2)}, u32[]{:S(2)}) collective-permute-start(bf16[192,16]{0,1:T(8,128)(2,1)S(1)} %convert.31), channel_id=1, source_target_pairs={{0,44},{4,48},{8,52},{12,56},{16,60},{20,64},{24,68},{28,72},{32,7... | collective-permute-start | bytes 18440
  306.2 16.0 %collective-permute-start.11 = (bf16[192,16]{0,1:T(8,128)(2,1)S(1)}, bf16[192,16]{0,1:T(8,128)(2,1)S(1)}, u32[]{:S(2)}, u32[]{:S(2)}) collective-permute-start(bf16[192,16]{0,1:T(8,128)(2,1)S(1)} %convert.31), channel_id=1, source_target_pairs={{0,48},{4,52},{8,56},{12,60},{16,64},{20,68},{24,72},{28,76},{32,8... | collective-permute-start | bytes 18440
  313.1 12.9 %collective-permute-start.12 = (bf16[192,16]{0,1:T(8,128)(2,1)S(1)}, bf16[192,16]{0,1:T(8,128)(2,1)S(1)}, u32[]{:S(2)}, u32[]{:S(2)}) collective-permute-start(bf16[192,16]{0,1:T(8,128)(2,1)S(1)} %convert.31), channel_id=1, source_target_pairs={{0,52},{4,56},{8,60},{12,64},{16,68},{20,72},{24,76},{28,80},{32,8... | collective-permute-start | bytes 18440
  315.2 13.6 %collective-permute-start.13 = (bf16[192,16]{0,1:T(8,128)(2,1)S(1)}, bf16[192,16]{0,1:T(8,128)(2,1)S(1)}, u32[]{:S(2)}, u32[]{:S(2)}) collective-permute-start(bf16[192,16]{0,1:T(8,128)(2,1)S(1)} %convert.31), channel_id=1, source_target_pairs={{0,56},{4,60},{8,64},{12,68},{16,72},{20,76},{24,80},{28,84},{32,8... | collective-permute-start | bytes 18440
  318.7 14.5 %collective-permute-start.14 = (bf16[192,16]{0,1:T(8,128)(2,1)S(1)}, bf16[192,16]{0,1:T(8,128)(2,1)S(1)}, u32[]{:S(2)}, u32[]{:S(2)}) collective-permute-start(bf16[192,16]{0,1:T(8,128)(2,1)S(1)} %convert.31), channel_id=1, source_target_pairs={{0,60},{4,64},{8,68},{12,72},{16,76},{20,80},{24,84},{28,88},{32,9... | collective-permute-start | bytes 18440
  320.1 14.5 %collective-permute-start.2 = (bf16[192,16]{0,1:T(8,128)(2,1)S(1)}, bf16[192,16]{0,1:T(8,128)(2,1)S(1)}, u32[]{:S(2)}, u32[]{:S(2)}) collective-permute-start(bf16[192,16]{0,1:T(8,128)(2,1)S(1)} %convert.31), channel_id=1, source_target_pairs={{0,12},{4,16},{8,20},{12,24},{16,28},{20,32},{24,36},{28,40},{32,4... | collective-permute-start | bytes 18440
  322.2 13.6 %collective-permute-start.3 = (bf16[192,16]{0,1:T(8,128)(2,1)S(1)}, bf16[192,16]{0,1:T(8,128)(2,1)S(1)}, u32[]{:S(2)}, u32[]{:S(2)}) collective-permute-start(bf16[192,16]{0,1:T(8,128)(2,1)S(1)} %convert.31), channel_id=1, source_target_pairs={{0,16},{4,20},{8,24},{12,28},{16,32},{20,36},{24,40},{28,44},{32,4... | collective-permute-start | bytes 18440
  326.0 12.3 %collective-permute-start.4 = (bf16[192,16]{0,1:T(8,128)(2,1)S(1)}, bf16[192,16]{0,1:T(8,128)(2,1)S(1)}, u32[]{:S(2)}, u32[]{:S(2)}) collective-permute-start(bf16[192,16]{0,1:T(8,128)(2,1)S(1)} %convert.31), channel_id=1, source_target_pairs={{0,20},{4,24},{8,28},{12,32},{16,36},{20,40},{24,44},{28,48},{32,5... | collective-permute-start | bytes 18440
  328.8 15.4 %collective-permute-start.5 = (bf16[192,16]{0,1:T(8,128)(2,1)S(1)}, bf16[192,16]{0,1:T(8,128)(2,1)S(1)}, u32[]{:S(2)}, u32[]{:S(2)}) collective-permute-start(bf16[192,16]{0,1:T(8,128)(2,1)S(1)} %convert.31), channel_id=1, source_target_pairs={{0,24},{4,28},{8,32},{12,36},{16,40},{20,44},{24,48},{28,52},{32,5... | collective-permute-start | bytes 18440
  333.2 11.0 %collective-permute-start.6 = (bf16[192,16]{0,1:T(8,128)(2,1)S(1)}, bf16[192,16]{0,1:T(8,128)(2,1)S(1)}, u32[]{:S(2)}, u32[]{:S(2)}) collective-permute-start(bf16[192,16]{0,1:T(8,128)(2,1)S(1)} %convert.31), channel_id=1, source_target_pairs={{0,28},{4,32},{8,36},{12,40},{16,44},{20,48},{24,52},{28,56},{32,6... | collective-permute-start | bytes 18440
  334.5 9.7 %collective-permute-start.7 = (bf16[192,16]{0,1:T(8,128)(2,1)S(1)}, bf16[192,16]{0,1:T(8,128)(2,1)S(1)}, u32[]{:S(2)}, u32[]{:S(2)}) collective-permute-start(bf16[192,16]{0,1:T(8,128)(2,1)S(1)} %convert.31), channel_id=1, source_target_pairs={{0,32},{4,36},{8,40},{12,44},{16,48},{20,52},{24,56},{28,60},{32,6... | collective-permute-start | bytes 18440
  335.9 8.4 %collective-permute-start.8 = (bf16[192,16]{0,1:T(8,128)(2,1)S(1)}, bf16[192,16]{0,1:T(8,128)(2,1)S(1)}, u32[]{:S(2)}, u32[]{:S(2)}) collective-permute-start(bf16[192,16]{0,1:T(8,128)(2,1)S(1)} %convert.31), channel_id=1, source_target_pairs={{0,36},{4,40},{8,44},{12,48},{16,52},{20,56},{24,60},{28,64},{32,6... | collective-permute-start | bytes 18440
  338.3 5.9 collective-permute-start.9
  340.3 2.0 copy-start.12
  353.7 1.9 copy-start.3
  (1 other events, 0.9 us)
Sparse Core Ops, SparseCore 0:
  192.3 50.9 all-reduce.9
  245.9 27.8 reduce-scatter.6
where the time goes:
time: 655 us; the launch traced here: 647 us
  blocking collectives  394 us (60%)
  local copies, waits for them, and re-layouts  89.8 us (14%)
  starting transfers between devices  68.4 us (10%)
  other arithmetic  32 us (5%)
  matrix products  27.7 us (4%)
  waiting for transfers between devices  19.7 us (3%)
  between operations  16.2 us (2%)
    unnamed x2, blocking collectives  331 us
    unnamed x17, starting transfers between devices  45.5 us
    unnamed x42, local copies, waits for them, and re-layouts  44.3 us
    all_to_all x1, blocking collectives, body(): lax.all_to_all(packed_cot_places, 'tm', split_axis=0, concat_axis=1, tile...  40 us
    all_to_all x1, blocking collectives, body(): lax.all_to_all(mixed_places, 'tm', split_axis=0, concat_axis=1, tiled=True)  22.9 us
    all_to_all x1, waiting for transfers between devices, body(): lax.all_to_all(packed, 'tm', split_axis=1, concat_axis=0, tiled=True)  19.6 us
    unnamed x3, other arithmetic  16 us
  transfers between devices with their start and end apart: 20, of which 1 were waited for; matrix products, arithmetic and copies ran while one was open for 21% of the time, Pallas kernels for 0%

commit v1 on v0

v1 whole, which is shorter than its diff:
```python
import jax
import jax.numpy as jnp
from jax import lax
from jax.experimental import pallas as pl
from jax.experimental.pallas import tpu as pltpu
from jax.sharding import PartitionSpec as P

MESH = pl.DeviceIdType.MESH
BF = jnp.bfloat16
F32 = jnp.float32
D = 768
EPS = 1e-05


def dot(a, b):
    return lax.dot_general(a, b, (((1,), (0,)), ((), ())), preferred_element_type=F32)


def dot_nt(a, b):
    return lax.dot_general(a, b, (((1,), (1,)), ((), ())), preferred_element_type=F32)


def dot_tn(a, b):
    return lax.dot_general(a, b, (((0,), (0,)), ((), ())), preferred_element_type=F32)


def iota(shape, axis):
    return lax.broadcasted_iota(jnp.int32, shape, axis)


def row_transpose_matrix():
    row = iota((256, 256), 0)
    col = iota((256, 256), 1)
    source = (row & 15) * 16 + (row >> 4)
    return jnp.where(col == source, 1.0, 0.0).astype(BF)


def feature_order_matrix():
    row = iota((D, 1), 0)
    core = (row >= 384).astype(jnp.int32)
    rest = row - 384 * core
    y = sum((rest >= 96 * k).astype(jnp.int32) for k in range(1, 4))
    rest = rest - 96 * y
    z = sum((rest >= 12 * k).astype(jnp.int32) for k in range(1, 8))
    rest = rest - 12 * z
    source = 12 * (z * 8 + y * 2 + core) + rest
    return jnp.where(iota((D, D), 1) == source, 1.0, 0.0).astype(BF)


def spread_matrix():
    row = iota((128, 96), 0)
    col = iota((128, 96), 1)
    inner = row & 15
    return jnp.where((inner < 12) & (col == (row >> 4) * 12 + inner), 1.0, 0.0).astype(BF)


def kernel(
    fr, ct, gain, w, runs,
    o_bo, o_gi, o_g, o_gg,
    r1, s2, r2, wb, std, nt, ctt, ncot, br, kept, pcm, gb, gc, hb, gx, hy, gy, gzs, gz,
    rb, t1, t2, ot, vg, vgc, vgx, vgy, vgz,
    a_s, a_r, b_s, b_r, w_s, w_r, f_s, f_r, c_s, c_r, x_s, x_r, y_s, y_r, z_s, z_r,
    p_s, p_r, q_s, q_r, vc_s, vc_r, vx_s, vx_r, vy_s, vy_r, vz_s, vz_r, l_s,
):
    m = lax.axis_index("tm")
    x = lax.axis_index("tensor")
    z = m // 8
    y = lax.rem(m // 2, 4)
    c = lax.rem(m, 2)
    me_zc = z * 2 + c

    def zc_peer(k):
        s = lax.rem(me_zc + k, 16)
        return s, ((s // 2) * 8 + y * 2 + lax.rem(s, 2), x)

    def yx_peer(k):
        q = lax.rem(x * 4 + y + k, 16)
        yy, xx = lax.rem(q, 4), q // 4
        return yy, xx, (z * 8 + yy * 2 + c, xx)

    def x_peer(k):
        xx = lax.rem(x + k, 4)
        return xx, (m, xx)

    def y_peer(k):
        yy = lax.rem(y + k, 4)
        return yy, (z * 8 + yy * 2 + c, x)

    def z_peer(k):
        zz = lax.rem(z + k, 8)
        return zz, (zz * 8 + y * 2 + c, x)

    core_peer = (z * 8 + y * 2 + (1 - c), x)

    def remote(src, dst, ss, rs, dev):
        return pltpu.make_async_remote_copy(
            src_ref=src, dst_ref=dst, send_sem=ss, recv_sem=rs, device_id=dev, device_id_type=MESH
        )

    def each(first, last, body):
        def step(k, carry):
            body(k)
            return carry
        lax.fori_loop(first, last, step, 0)

    barrier = pltpu.get_barrier_semaphore()

    def greet_zc(k):
        pl.semaphore_signal(barrier, inc=1, device_id=zc_peer(k)[1], device_id_type=MESH)

    def greet_yx(k):
        pl.semaphore_signal(barrier, inc=1, device_id=yx_peer(k)[2], device_id_type=MESH)

    each(1, 16, greet_zc)
    each(1, 16, greet_yx)

    own_w = pltpu.make_async_copy(w, wb.at[x], l_s.at[0])
    own_w.start()

    def own_rows(k):
        ref = (fr, ct)[k]
        return pltpu.make_async_copy(
            ref.at[pl.ds((me_zc * 4 + x) * 16, 16)], r1.at[k, me_zc], l_s.at[1 + k]
        )

    own_rows(0).start()
    own_rows(1).start()
    pl.semaphore_wait(barrier, 30)

    def token_copy(k, n):
        s, dev = zc_peer(n)
        rows = pl.ds((s * 4 + x) * 16, 16)
        return remote((fr, ct)[k].at[rows], r1.at[k, me_zc], a_s.at[k, s], a_r.at[k, me_zc], dev)

    def send_tokens(n):
        token_copy(0, n).start()
        token_copy(1, n).start()

    each(1, 16, send_tokens)

    half = pl.ds(c * 384, 384)

    def weight_copy(n):
        xx, dev = x_peer(n)
        return remote(w.at[half], wb.at[x, half], w_s.at[xx], w_r.at[x], dev)

    for n in (1, 3, 2):
        weight_copy(n).start()

    turn = row_transpose_matrix()
    order = feature_order_matrix()
    spread = spread_matrix()

    begin, end = runs[0], runs[1]
    for i in range(4):
        place = (me_zc * 4 + x) * 16 + y * 4 + i
        inside = jnp.where((begin <= place) & (place < end), 1.0, 0.0)
        kept[pl.ds(64 * i, 64), :] = jnp.broadcast_to(jnp.sum(inside, axis=1, keepdims=True), (64, 128))

    def got_tokens(n):
        s = lax.rem(me_zc + n, 16)
        for k in range(2):
            remote(fr.at[pl.ds(0, 16)], r1.at[k, s], a_s.at[k, s], a_r.at[k, s], core_peer).wait_recv()

    each(1, 16, got_tokens)
    own_rows(0).wait()
    own_rows(1).wait()
    for k in range(2):
        turned = dot(turn, r1[k].reshape(256, D)).astype(BF).reshape(4, 4, 16, D)
        s2[k] = turned

    def group_copy(n):
        yy, dev = y_peer(n)
        return remote(s2.at[:, yy], r2.at[:, :, y], b_s.at[yy], b_r.at[y], dev)

    for n in (1, 3, 2):
        group_copy(n).start()
    own_group = pltpu.make_async_copy(s2.at[:, y], r2.at[:, :, y], l_s.at[3])
    own_group.start()

    def forward_copy(n):
        xx = lax.rem(x + n, 4)
        return remote(wb.at[xx, half], wb.at[xx, half], f_s.at[xx], f_r.at[xx], core_peer)

    other_half = pl.ds((1 - c) * 384, 384)

    for n in (1, 3, 2):
        xx = lax.rem(x + n, 4)
        remote(w.at[half], wb.at[xx, half], w_s.at[xx], w_r.at[xx], core_peer).wait_recv()
        forward_copy(n).start()
    own_w.wait()

    for n in (1, 3, 2):
        yy = lax.rem(y + n, 4)
        remote(s2.at[:, yy], r2.at[:, :, yy], b_s.at[yy], b_r.at[yy], core_peer).wait_recv()
    own_group.wait()

    tokens = r2[0].reshape(256, D).astype(F32)
    centre = jnp.mean(tokens, axis=-1, keepdims=True)
    shifted = tokens - centre
    inverse = lax.rsqrt(jnp.mean(shifted * shifted, axis=-1, keepdims=True) + EPS)
    standard = shifted * inverse
    std[...] = standard
    normed = (standard * gain[...]).astype(BF)
    pcm[1] = normed
    nt[...] = dot_nt(order, normed).astype(BF)
    ctt[...] = dot_nt(order, r2[1].reshape(256, D)).astype(BF)
    ncot[...] = jnp.zeros((256, D), F32)
    br[...] = jnp.zeros((256, D), F32)

    lane = iota((64, 192), 1)
    head_mask = [(lane >= 64 * h) & (lane < 64 * h + 64) for h in range(3)]

    def stack_heads(rows):
        return jnp.concatenate([jnp.where(hm, rows, jnp.zeros_like(rows)) for hm in head_mask], axis=0)

    def pick_heads(rows):
        return jnp.where(head_mask[0], rows[0:64], jnp.where(head_mask[1], rows[64:128], rows[128:192]))

    def finish_core(jj):
        remote(gb.at[jj, c], gc.at[jj], c_s.at[jj], c_r.at[jj], core_peer).wait_recv()
        hb[jj] = (gb[jj, c].astype(F32) + gc[jj].astype(F32)).astype(BF)

    def share_copy(jj):
        xx, dev = x_peer(jj + 1)
        return remote(hb.at[jj], gx.at[x], x_s.at[xx], x_r.at[x], dev)

    def core_copy(jj):
        return remote(gb.at[jj, 1 - c], gc.at[jj], c_s.at[jj], c_r.at[jj], core_peer)

    def heads_step(jj, carry):
        j = lax.rem(x + jj + 1, 4)

        @pl.when(jj < 3)
        def _():
            remote(wb.at[j, other_half], wb.at[j, other_half], f_s.at[j], f_r.at[j], core_peer).wait_recv()

        packed = dot(pcm[1], wb[j]).astype(BF)
        cot = dot(r2[1].reshape(256, D), wb[j, :, 512:768]).astype(BF)[:, 64:256]
        for i in range(4):
            rows = slice(64 * i, 64 * i + 64)
            keep = kept[rows, 0:1] > 0
            keep3 = jnp.concatenate([kept[rows, 0:1]] * 3, axis=0) > 0
            q = packed[rows, 0:192]
            kk = packed[rows, 192:384]
            v = packed[rows, 384:576]
            mc = jnp.where(keep, cot[rows], jnp.zeros((64, 192), BF))
            kbd = stack_heads(kk)
            vbd = stack_heads(v)
            scores = jnp.where(keep3, dot_nt(kbd, q) * 0.125, -1000000000.0).reshape(3, 64, 64)
            top = jnp.max(scores, axis=1, keepdims=True)
            expo = jnp.exp(scores - top)
            weight = expo / jnp.sum(expo, axis=1, keepdims=True)
            wbf = weight.astype(BF).reshape(192, 64)
            mixed = jnp.where(keep, dot_tn(wbf, vbd), 0.0).astype(BF)
            dweight = dot_nt(vbd, mc).reshape(3, 64, 64)
            inner = jnp.sum(dweight * weight, axis=1, keepdims=True)
            dscore = (weight * (dweight - inner) * 0.125).astype(BF).reshape(192, 64)
            dq = dot_tn(dscore, kbd).astype(BF)
            dk = pick_heads(dot(dscore, q)).astype(BF)
            dv = pick_heads(dot(wbf, mc)).astype(BF)
            pcm[0, rows, 0:192] = dq
            pcm[0, rows, 192:384] = dk
            pcm[0, rows, 384:576] = dv
            pcm[0, rows, 576:768] = mixed
        low = iota((256, 256), 1) < 64
        tail = pcm[0, :, 512:768]
        tail_qkv = jnp.where(low, tail, jnp.zeros_like(tail))
        tail_mix = jnp.where(low, jnp.zeros_like(tail), tail)
        for h in range(2):
            rows = slice(384 * h, 384 * h + 384)
            gb[jj, h, :, 0:512] = dot(nt[rows, :], pcm[0, :, 0:512]).astype(BF)
            gb[jj, h, :, 512:768] = (dot(nt[rows, :], tail_qkv) + dot(ctt[rows, :], tail_mix)).astype(BF)
        core_copy(jj).start()
        wj_tail = wb[j, :, 512:768]
        ncot[...] += dot_nt(pcm[0, :, 0:512], wb[j, :, 0:512]) + dot_nt(tail_qkv, wj_tail)
        br[...] += dot_nt(tail_mix, wj_tail)

        @pl.when(jj > 0)
        def _():
            finish_core(jj - 1)
            share_copy(jj - 1).start()

        return carry

    lax.fori_loop(0, 4, heads_step, 0)

    block = (r2[0].reshape(256, D).astype(F32) + br[...]).astype(BF)
    cotangent = ncot[...].astype(BF).astype(F32)
    standard = std[...]
    scaled = cotangent * gain[...]
    mean_plain = jnp.mean(scaled, axis=-1, keepdims=True)
    mean_cross = jnp.mean(scaled * standard, axis=-1, keepdims=True)
    tokens = r2[0].reshape(256, D).astype(F32)
    centre = jnp.mean(tokens, axis=-1, keepdims=True)
    shifted = tokens - centre
    inverse = lax.rsqrt(jnp.mean(shifted * shifted, axis=-1, keepdims=True) + EPS)
    through = inverse * (scaled - mean_plain - standard * mean_cross)
    grad_in = (r2[1].reshape(256, D).astype(F32) + through).astype(BF)
    for xx in range(4):
        cols = slice(192 * xx, 192 * xx + 192)
        rb[xx] = jnp.concatenate([block[:, cols], grad_in[:, cols]], axis=1).reshape(4, 4, 16, 384)

    def result_copy(n):
        yy, xx, dev = yx_peer(n)
        return remote(rb.at[xx, :, yy], t1.at[x, y], p_s.at[xx, yy], p_r.at[x, y], dev)

    def send_result(n):
        result_copy(n).start()

    each(1, 16, send_result)
    own_result = pltpu.make_async_copy(rb.at[x, :, y], t1.at[x, y], l_s.at[4])
    own_result.start()

    gain_part = jnp.sum(cotangent * standard, axis=0, keepdims=True)
    vg[0] = jnp.concatenate(
        [gain_part[:, 192 * k : 192 * k + 192] for k in range(4)] + [jnp.zeros((4, 192), F32)], axis=0
    )
    gain_core = remote(vg.at[0], vgc, vc_s, vc_r, core_peer)
    gain_core.start()
    finish_core(3)
    gain_core.wait_recv()
    vg[1] = vg[0] + vgc[...]

    def gain_x(n):
        xx, dev = x_peer(n)
        return remote(vg.at[1], vgx.at[x], vx_s.at[xx], vx_r.at[x], dev)

    for n in range(1, 4):
        gain_x(n).start()

    own_result.wait()

    def place_copy(xx, n):
        s, dev = zc_peer(n)
        return remote(
            t2.at[xx, s], ot.at[me_zc, xx], q_s.at[xx, s], q_r.at[xx, me_zc], dev
        )

    def own_place(xx):
        return pltpu.make_async_copy(t2.at[xx, me_zc], ot.at[me_zc, xx], l_s.at[5 + xx])

    def group_step(n, carry):
        xx = lax.rem(x + n, 4)

        def got(k):
            yy = lax.rem(y + k, 4)

            @pl.when((n > 0) | (k > 0))
            def _():
                remote(rb.at[xx, :, yy], t1.at[xx, yy], p_s.at[xx, yy], p_r.at[xx, yy], core_peer).wait_recv()

        each(0, 4, got)
        t2[xx] = dot(turn, t1[xx].reshape(256, 384)).astype(BF).reshape(16, 16, 384)
        each(1, 16, lambda k: place_copy(xx, k).start())
        own_place(xx).start()
        return carry

    lax.fori_loop(0, 4, group_step, 0)

    total = hb[3].astype(F32)
    for n in range(1, 4):
        xx = lax.rem(x + n, 4)
        remote(hb.at[0], gx.at[xx], x_s.at[xx], x_r.at[xx], core_peer).wait_recv()
        total = total + gx[xx].astype(F32)
    hy[...] = total.astype(BF).reshape(4, 96, D)
    gain_total = vg[1]
    for n in range(1, 4):
        xx = lax.rem(x + n, 4)
        remote(vg.at[1], vgx.at[xx], vx_s.at[xx], vx_r.at[xx], core_peer).wait_recv()
        gain_total = gain_total + vgx[xx]
    vg[2] = gain_total

    def grad_y(n):
        yy, dev = y_peer(n)
        return remote(hy.at[yy], gy.at[y], y_s.at[yy], y_r.at[y], dev)

    def gain_y(n):
        yy, dev = y_peer(n)
        return remote(vg.at[2], vgy.at[y], vy_s.at[yy], vy_r.at[y], dev)

    for n in range(1, 4):
        grad_y(n).start()
        gain_y(n).start()
    total = hy[y].astype(F32)
    gain_total = vg[2]
    for n in range(1, 4):
        yy = lax.rem(y + n, 4)
        remote(hy.at[yy], gy.at[yy], y_s.at[yy], y_r.at[yy], core_peer).wait_recv()
        remote(vg.at[2], vgy.at[yy], vy_s.at[yy], vy_r.at[yy], core_peer).wait_recv()
        total = total + gy[yy].astype(F32)
        gain_total = gain_total + vgy[yy]
    gzs[...] = dot(spread, total.astype(BF)).astype(BF).reshape(8, 16, D)
    vg[3] = gain_total

    def grad_z(n):
        zz, dev = z_peer(n)
        return remote(gzs.at[zz], gz.at[z], z_s.at[zz], z_r.at[z], dev)

    def gain_z(n):
        zz, dev = z_peer(n)
        return remote(vg.at[3], vgz.at[z], vz_s.at[zz], vz_r.at[z], dev)

    for n in range(1, 8):
        grad_z(n).start()
        gain_z(n).start()
    total = gzs[z].astype(F32)
    gain_total = vg[3]
    for n in range(1, 8):
        zz = lax.rem(z + n, 8)
        remote(gzs.at[zz], gz.at[zz], z_s.at[zz], z_r.at[zz], core_peer).wait_recv()
        remote(vg.at[3], vgz.at[zz], vz_s.at[zz], vz_r.at[zz], core_peer).wait_recv()
        total = total + gz[zz].astype(F32)
        gain_total = gain_total + vgz[zz]
    o_g[...] = total.astype(BF)
    o_gg[...] = jnp.sum(jnp.where(iota((8, 192), 0) == x, gain_total, 0.0), axis=0, keepdims=True)

    def placed(xx):
        own_place(xx).wait()

        def one(k):
            s = lax.rem(me_zc + k, 16)
            remote(t2.at[xx, s], ot.at[s, xx], q_s.at[xx, s], q_r.at[xx, s], core_peer).wait_recv()

        each(1, 16, one)

    each(0, 4, placed)
    results = ot[...].reshape(1024, 384)
    o_bo[...] = results[:, 0:192]
    o_gi[...] = results[:, 192:384]

    def sent_zc(n):
        token_copy(0, n).wait_send()
        token_copy(1, n).wait_send()
        result_copy(n).wait_send()
        each(0, 4, lambda xx: place_copy(xx, n).wait_send())

    each(1, 16, sent_zc)
    for n in range(1, 4):
        weight_copy(n).wait_send()
        forward_copy(n).wait_send()
        group_copy(n).wait_send()
        gain_x(n).wait_send()
        grad_y(n).wait_send()
        gain_y(n).wait_send()
    each(0, 4, lambda jj: core_copy(jj).wait_send())
    each(0, 3, lambda jj: share_copy(jj).wait_send())
    for n in range(1, 8):
        grad_z(n).wait_send()
        gain_z(n).wait_send()
    gain_core.wait_send()


def body(frames_in, norm_gain, w_qkv, w_out, keep_runs, out_cotangent):
    w_all = jnp.concatenate([w_qkv.reshape(D, 576), w_out.T], axis=1)
    runs = keep_runs.reshape(8, 4, 2, 16, 2).transpose(4, 1, 0, 2, 3).reshape(2, 64, 16)
    runs = jnp.stack([runs[0], runs[0] + runs[1]])
    v = lambda shape, dt=BF: pltpu.VMEM(shape, dt)
    dma = pltpu.SemaphoreType.DMA
    any_spec = pl.BlockSpec(memory_space=pl.ANY)
    vmem_spec = pl.BlockSpec(memory_space=pltpu.VMEM)
    block_out, grad_in, grads, grad_gain = pl.pallas_call(
        kernel,
        out_shape=(
            jax.ShapeDtypeStruct((1024, 192), BF),
            jax.ShapeDtypeStruct((1024, 192), BF),
            jax.ShapeDtypeStruct((16, D), BF),
            jax.ShapeDtypeStruct((1, 192), F32),
        ),
        in_specs=[any_spec, any_spec, vmem_spec, any_spec, vmem_spec],
        out_specs=(vmem_spec,) * 4,
        scratch_shapes=[
            v((2, 16, 16, D)),
            v((2, 4, 4, 16, D)),
            v((2, 4, 4, 16, D)),
            v((4, D, D)),
            v((256, D), F32),
            v((D, 256)),
            v((D, 256)),
            v((256, D), F32),
            v((256, D), F32),
            v((256, 128), F32),
            v((2, 256, D)),
            v((4, 2, 384, D)),
            v((4, 384, D)),
            v((4, 384, D)),
            v((4, 384, D)),
            v((4, 96, D)),
            v((4, 96, D)),
            v((8, 16, D)),
            v((8, 16, D)),
            v((4, 4, 4, 16, 384)),
            v((4, 4, 4, 16, 384)),
            v((4, 16, 16, 384)),
            v((16, 4, 16, 384)),
            v((4, 8, 192), F32),
            v((8, 192), F32),
            v((4, 8, 192), F32),
            v((4, 8, 192), F32),
            v((8, 8, 192), F32),
            dma((2, 16)), dma((2, 16)),
            dma((4,)), dma((4,)),
            dma((4,)), dma((4,)),
            dma((4,)), dma((4,)),
            dma((4,)), dma((4,)),
            dma((4,)), dma((4,)),
            dma((4,)), dma((4,)),
            dma((8,)), dma((8,)),
            dma((4, 4)), dma((4, 4)),
            dma((4, 16)), dma((4, 16)),
            dma(()), dma(()),
            dma((4,)), dma((4,)),
            dma((4,)), dma((4,)),
            dma((8,)), dma((8,)),
            dma((9,)),
        ],
        compiler_params=pltpu.CompilerParams(
            collective_id=0, has_side_effects=True, vmem_limit_bytes=56 << 20
        ),
        cost_estimate=pl.CostEstimate(flops=5 * 10**9, bytes_accessed=10**7, transcendentals=200000),
        name="block",
    )(
        frames_in.reshape(1024, D), out_cotangent.reshape(1024, D), norm_gain.reshape(1, D), w_all, runs
    )
    return (
        block_out.reshape(1, 1024, 192),
        grad_in.reshape(1, 1024, 192),
        grads[:12, :576].reshape(12, 3, 192),
        grads[:12, 576:].T,
        grad_gain.reshape(192),
    )


def solution(mesh):
    in_specs = (
        P("tm", None, None),
        P(),
        P(None, None, "tensor"),
        P("tensor", None),
        P(),
        P("tm", None, None),
    )
    out_specs = (
        P("tm", None, "tensor"),
        P("tm", None, "tensor"),
        P("tm", None, "tensor"),
        P("tensor", "tm"),
        P("tensor"),
    )
    return jax.shard_map(body, mesh=mesh, in_specs=in_specs, out_specs=out_specs, check_vma=False)
```

time: 655 us -> 132 us (0.20); the launches traced: 647 us -> 132 us
  blocking collectives: 394 us -> 0 us
  Pallas kernels: 0 us -> 119 us
  local copies, waits for them, and re-layouts: 89.8 us -> 9.97 us
  starting transfers between devices: 68.4 us -> 0 us
  other arithmetic: 32 us -> 1.87 us
  matrix products: 27.7 us -> 0 us
  waiting for transfers between devices: 19.7 us -> 0 us
  between operations: 16.2 us -> 0.71 us
    unnamed x2 -> x0, blocking collectives: 331 us -> none
    pallas_call x0 -> x1, Pallas kernels: none -> 119 us  [body(): pl.pallas_call(kernel, out_shape=(jax.ShapeDtypeStruct((1024, 192), BF),...]
    all_to_all x2 -> x0, blocking collectives: 62.9 us -> none  [the longest x1 40 us: body(): lax.all_to_all(packed_cot_places, 'tm', split_axis=0, concat_axis=1, tile...]
    unnamed x17 -> x0, starting transfers between devices: 45.5 us -> none
    unnamed x42 -> x11, local copies, waits for them, and re-layouts: 44.3 us -> 5.75 us
    dot_general x12 -> x0, matrix products: 27.7 us -> none  [the longest x2 7.51 us: contract_rows(): lax.dot_general(left.reshape(-1, left.shape[-1]), right.reshape(-1, right...]
    all_to_all x2 -> x0, starting transfers between devices: 22.9 us -> none  [the longest x1 12.3 us: body(): lax.all_to_all(mixed_cot, 'tm', split_axis=1, concat_axis=0, tiled=True)]
    all_to_all x2 -> x0, waiting for transfers between devices: 19.6 us -> none  [the longest x1 19.6 us: body(): lax.all_to_all(packed, 'tm', split_axis=1, concat_axis=0, tiled=True)]
  transfers between devices with their start and end apart: 20 -> 0, of which waited for: 1 -> 0; matrix products, arithmetic and copies ran while one was open for 21% -> 0% of each run, Pallas kernels for 0% -> 0%
where the time goes in v1:
time: 132 us
  Pallas kernels  119 us (90%)
  local copies, waits for them, and re-layouts  9.97 us (8%)
  other arithmetic  1.87 us (1%)
    pallas_call x1, Pallas kernels, body(): pl.pallas_call(kernel, out_shape=(jax.ShapeDtypeStruct((1024, 192), BF),...  119 us
    unnamed x11, local copies, waits for them, and re-layouts  5.75 us

profile of v1, /device:TPU:2, one launch (start us, length us, event | category | flops | bytes accessed | tf_op | source)
XLA Modules:
  0.0 131.7 jit_solution(17534009677749727008)
XLA Ops:
  0.6 1.3 reshape.61.gain
  1.9 1.1 copy.39
  3.0 1.5 %copy.40 = bf16[768,576]{1,0:T(8,128)(2,1)S(1)} copy(bf16[768,576]{0,1:T(8,128)(2,1)} %bitcast.15) | data formatting | bytes 1769472 | tf_op jit(solution)/shard_map/reshape | solution.py:455
  4.6 0.0 copy-start.1
  4.6 1.2 pad_maximum_fusion.w
  5.8 0.0 copy-done.1
  5.8 0.1 copy.41
  6.0 0.6 pad_add_fusion.runs
  6.6 119.1 %block.1 = (bf16[1024,192]{1,0:T(8,128)(2,1)}, bf16[1024,192]{1,0:T(8,128)(2,1)}, bf16[16,768]{1,0:T(8,128)(2,1)}, f32[1,192]{1,0:T(1,128)}) custom-call(bf16[1024,768]{1,0:T(8,128)(2,1)} %bitcast.23, bf16[1024,768]{1,0:T(8,128)(2,1)} %bitcast.24, f32[1,768]{1,0:T(1,128)} %reshape.61.gain, bf16[768,768]{1,0:T(8,128)(2,1)} %pad_maximum_fusion.w, ...), custom_call_target="tpu_custom_call" | custom-call | flops 5000000000 | bytes 10000000 | tf_op jit(solution)/shard_map/block/pallas_call | solution.py:462
  125.7 0.0 copy-start
  125.7 0.0 copy-start.2
  125.8 2.0 %copy.44 = bf16[1,1024,192]{1,2,0:T(8,128)(2,1)} copy(bf16[1,1024,192]{2,1,0:T(8,128)(2,1)} %bitcast.17) | data formatting | bytes 786432
  127.7 2.0 %copy.45 = bf16[1,1024,192]{1,2,0:T(8,128)(2,1)} copy(bf16[1,1024,192]{2,1,0:T(8,128)(2,1)} %bitcast.16) | data formatting | bytes 786432
  129.7 0.0 copy-done
  129.7 0.7 reshape.66
  130.4 0.7 slice_bitcast_fusion
  131.1 0.0 copy-done.2
  131.1 0.6 copy.47
  (5 shorter events, 0.0 us)
Async XLA Ops:
  4.6 1.2 copy-start.1
  125.7 4.0 %copy-start = (bf16[16,768]{1,0:T(8,128)(2,1)S(1)}, bf16[16,768]{1,0:T(8,128)(2,1)}, u32[]{:S(2)}) copy-start(bf16[16,768]{1,0:T(8,128)(2,1)} %get-tuple-element.11) | copy-start | bytes 73732
  125.7 5.4 %copy-start.2 = (f32[1,192]{1,0:T(1,128)S(1)}, f32[1,192]{1,0:T(1,128)}, u32[]{:S(2)}) copy-start(f32[1,192]{1,0:T(1,128)} %get-tuple-element.12) | copy-start | bytes 2308

commit v2 on v1

v2 whole, which is shorter than its diff:
```python
import jax
import jax.numpy as jnp
from jax import lax
from jax.experimental import pallas as pl
from jax.experimental.pallas import tpu as pltpu
from jax.sharding import PartitionSpec as P

MESH = pl.DeviceIdType.MESH
BF = jnp.bfloat16
F32 = jnp.float32
D = 768
EPS = 1e-05


def dot(a, b):
    return lax.dot_general(a, b, (((1,), (0,)), ((), ())), preferred_element_type=F32)


def dot_nt(a, b):
    return lax.dot_general(a, b, (((1,), (1,)), ((), ())), preferred_element_type=F32)


def dot_tn(a, b):
    return lax.dot_general(a, b, (((0,), (0,)), ((), ())), preferred_element_type=F32)


def iota(shape, axis):
    return lax.broadcasted_iota(jnp.int32, shape, axis)


def row_transpose_matrix():
    row = iota((256, 256), 0)
    col = iota((256, 256), 1)
    source = (row & 15) * 16 + (row >> 4)
    return jnp.where(col == source, 1.0, 0.0).astype(BF)


def feature_order_matrix():
    row = iota((D, 1), 0)
    core = (row >= 384).astype(jnp.int32)
    rest = row - 384 * core
    y = sum((rest >= 96 * k).astype(jnp.int32) for k in range(1, 4))
    rest = rest - 96 * y
    z = sum((rest >= 12 * k).astype(jnp.int32) for k in range(1, 8))
    rest = rest - 12 * z
    source = 12 * (z * 8 + y * 2 + core) + rest
    return jnp.where(iota((D, D), 1) == source, 1.0, 0.0).astype(BF)


def spread_matrix():
    row = iota((128, 96), 0)
    col = iota((128, 96), 1)
    inner = row & 15
    return jnp.where((inner < 12) & (col == (row >> 4) * 12 + inner), 1.0, 0.0).astype(BF)


def frame_order_matrix():
    row = iota((64, 64), 0)
    source = ((row >> 1) & 7) * 8 + (row >> 4) * 2 + (row & 1)
    return jnp.where(iota((64, 64), 1) == source, 1.0, 0.0).astype(BF)


def unpair_matrix():
    row = iota((256, 256), 0)
    col = iota((256, 256), 1)
    return jnp.where(col == (row & 127) * 2 + (row >> 7), 1.0, 0.0).astype(BF)


def kernel(
    fr, ct, gain, wq, wo, runs,
    o_bo, o_gi, o_gq, o_gp, o_gg,
    r1, s2, r2, wb, std, inv, nrm, nt, ctt, ncot, br, kept, keptw, qkv, wts, mx, pcm,
    gb, gc, hb, gx, gy1, hy1, gx2, hx, gy2, gzs, gz,
    rb, t1, t2, ot, vg, vgc, vgx, vgy, vgz,
    a_s, a_r, b_s, b_r, w_s, w_r, f_s, f_r, c_s, c_r, x_s, x_r, y1_s, y1_r, x2_s, x2_r,
    y2_s, y2_r, z_s, z_r, p_s, p_r, q_s, q_r, vc_s, vc_r, vx_s, vx_r, vy_s, vy_r, vz_s, vz_r, l_s,
):
    m = lax.axis_index("tm")
    x = lax.axis_index("tensor")
    z = m // 8
    y = lax.rem(m // 2, 4)
    c = lax.rem(m, 2)
    me_zc = z * 2 + c

    def zc_peer(k):
        s = lax.rem(me_zc + k, 16)
        return s, ((s // 2) * 8 + y * 2 + lax.rem(s, 2), x)

    def yx_peer(k):
        q = lax.rem(x * 4 + y + k, 16)
        yy, xx = lax.rem(q, 4), q // 4
        return yy, xx, (z * 8 + yy * 2 + c, xx)

    def x_peer(k):
        xx = lax.rem(x + k, 4)
        return xx, (m, xx)

    def y_peer(k):
        yy = lax.rem(y + k, 4)
        return yy, (z * 8 + yy * 2 + c, x)

    def z_peer(k):
        zz = lax.rem(z + k, 8)
        return zz, (zz * 8 + y * 2 + c, x)

    core_peer = (z * 8 + y * 2 + (1 - c), x)
    x_right, x_left, x_far = lax.rem(x + 1, 4), lax.rem(x + 3, 4), lax.rem(x + 2, 4)

    def remote(src, dst, ss, rs, dev):
        return pltpu.make_async_remote_copy(
            src_ref=src, dst_ref=dst, send_sem=ss, recv_sem=rs, device_id=dev, device_id_type=MESH
        )

    def arrive(dst, rs):
        remote(dst, dst, l_s.at[9], rs, core_peer).wait_recv()

    def each(first, last, body):
        def step(k, carry):
            body(k)
            return carry
        lax.fori_loop(first, last, step, 0)

    barrier = pltpu.get_barrier_semaphore()

    def greet(k):
        pl.semaphore_signal(barrier, inc=1, device_id=zc_peer(k)[1], device_id_type=MESH)
        pl.semaphore_signal(barrier, inc=1, device_id=yx_peer(k)[2], device_id_type=MESH)

    each(1, 16, greet)

    own_w = [
        pltpu.make_async_copy(wq, wb.at[x, pl.ds(0, 576)], l_s.at[0]),
        pltpu.make_async_copy(wo, wb.at[x, pl.ds(576, 192)], l_s.at[3]),
    ]
    for copy in own_w:
        copy.start()

    def own_rows(k):
        ref = (fr, ct)[k]
        return pltpu.make_async_copy(
            ref.at[pl.ds((me_zc * 4 + x) * 16, 16)], r1.at[k, me_zc], l_s.at[1 + k]
        )

    own_rows(0).start()
    own_rows(1).start()
    turn = row_transpose_matrix()
    pl.semaphore_wait(barrier, 30)

    def token_copy(k, n):
        s, dev = zc_peer(n)
        rows = pl.ds((s * 4 + x) * 16, 16)
        return remote((fr, ct)[k].at[rows], r1.at[k, me_zc], a_s.at[k, s], a_r.at[k, me_zc], dev)

    each(1, 16, lambda n: token_copy(0, n).start())
    for copy in own_w:
        copy.wait()

    def part(xx, half, ab):
        return wb.at[xx, pl.ds(half * 384 + ab * 192, 192)]

    def weight_copy(n):
        to_right = n in (0, 2, 4)
        xx = (x, x, x, x, x_left, x_right)[n]
        ab = (0, 1, 1, 0, 0, 1)[n]
        dev = (m, x_right if to_right else x_left)
        return remote(part(xx, c, ab), part(xx, c, ab), w_s.at[n], w_r.at[xx, ab], dev)

    for n in range(4):
        weight_copy(n).start()
    each(1, 16, lambda n: token_copy(1, n).start())

    def swap_copy(xx, ab):
        return remote(part(xx, c, ab), part(xx, c, ab), f_s.at[xx, ab], f_r.at[xx, ab], core_peer)

    def take_weights(xx, ab):
        arrive(part(xx, c, ab), w_r.at[xx, ab])
        swap_copy(xx, ab).start()

    order = feature_order_matrix()

    begin = runs[:, 0, :]
    end = begin + runs[:, 1, :]
    rows = []
    for i in range(4):
        place = (me_zc * 4 + x) * 16 + y * 4 + i
        inside = jnp.where((begin <= place) & (place < end), 1.0, 0.0)
        rows.append(jnp.sum(inside, axis=0, keepdims=True))
    rows = jnp.concatenate(rows + [jnp.zeros((4, 64), F32)], axis=0).astype(BF)
    columns = dot_nt(frame_order_matrix(), rows)
    for i in range(4):
        kept[pl.ds(64 * i, 64), :] = jnp.broadcast_to(columns[:, i : i + 1], (64, 128))
    first_of_pair = iota((64, 128), 1) < 64
    for p in range(2):
        keptw[p] = jnp.where(first_of_pair, kept[128 * p : 128 * p + 64, :], kept[128 * p + 64 : 128 * p + 128, :])

    def group_copy(k, n):
        yy, dev = y_peer(n)
        return remote(s2.at[k, yy], r2.at[k, :, y], b_s.at[k, yy], b_r.at[k, y], dev)

    def own_group(k):
        return pltpu.make_async_copy(s2.at[k, y], r2.at[k, :, y], l_s.at[4 + k])

    def regroup(k):
        each(1, 16, lambda n: arrive(r1.at[k, lax.rem(me_zc + n, 16)], a_r.at[k, lax.rem(me_zc + n, 16)]))
        own_rows(k).wait()
        s2[k] = dot(turn, r1[k].reshape(256, D)).astype(BF).reshape(4, 4, 16, D)
        for n in (1, 3, 2):
            group_copy(k, n).start()
        own_group(k).start()

    def grouped(k):
        for n in (1, 3, 2):
            yy = lax.rem(y + n, 4)
            arrive(r2.at[k, :, yy], b_r.at[k, yy])
        own_group(k).wait()

    regroup(0)
    take_weights(x_left, 0)
    weight_copy(4).start()
    take_weights(x_right, 1)
    weight_copy(5).start()
    grouped(0)

    tokens = r2[0].reshape(256, D).astype(F32)
    centre = jnp.mean(tokens, axis=-1, keepdims=True)
    shifted = tokens - centre
    inverse = lax.rsqrt(jnp.mean(shifted * shifted, axis=-1, keepdims=True) + EPS)
    standard = shifted * inverse
    std[...] = standard
    inv[...] = jnp.broadcast_to(inverse, (256, 128))
    gains = gain[...].reshape(1, D)
    normed = (standard * gains).astype(BF)
    nrm[...] = normed
    nt[...] = dot_nt(order, normed).astype(BF)
    ncot[...] = jnp.zeros((256, D), F32)
    br[...] = jnp.zeros((256, D), F32)

    lane = iota((64, 192), 1)
    head_mask = [(lane >= 64 * h) & (lane < 64 * h + 64) for h in range(3)]
    top_rows = iota((128, 192), 0) < 64
    nothing = jnp.zeros((128, 192), BF)

    def stack_heads(rows):
        return jnp.concatenate([jnp.where(hm, rows, jnp.zeros_like(rows)) for hm in head_mask], axis=0)

    def pick_heads(rows):
        return jnp.where(head_mask[0], rows[0:64], jnp.where(head_mask[1], rows[64:128], rows[128:192]))

    def only(rows, which):
        return jnp.where(top_rows, rows, nothing) if which == 0 else jnp.where(top_rows, nothing, rows)

    pairs = [slice(128 * p, 128 * p + 128) for p in range(2)]

    def forward_step(j):
        q, kk, v = [dot_nt(nrm[...], wb[j, 192 * n : 192 * n + 192, :]).astype(BF) for n in range(3)]
        qkv[j, 0], qkv[j, 1], qkv[j, 2] = q, kk, v
        kbd = [stack_heads(kk[64 * i : 64 * i + 64]) for i in range(4)]
        scores = [
            sum(dot_nt(kbd[2 * p + e], only(q[pairs[p]], e)) for e in range(2)) for p in range(2)
        ]
        vbd = [stack_heads(v[64 * i : 64 * i + 64]) for i in range(4)]
        weights = []
        for p in range(2):
            masked = jnp.where((keptw[p] > 0)[None], scores[p].reshape(3, 64, 128) * 0.125, -1000000000.0)
            top = jnp.max(masked, axis=1, keepdims=True)
            expo = jnp.exp(masked - top)
            weight = (expo / jnp.sum(expo, axis=1, keepdims=True)).reshape(192, 128)
            wts[j, p] = weight
            weights.append(weight.astype(BF))
        mixed = []
        for i in range(4):
            e = i % 2
            mixed.append(dot_tn(weights[i // 2], vbd[i])[64 * e : 64 * e + 64])
        mixed = jnp.concatenate(mixed, axis=0)
        mixed = jnp.where(kept[:, 0:1] > 0, mixed, 0.0).astype(BF)
        mx[j] = mixed
        br[...] += dot(mixed, wb[j, 576:768, :])

    forward_step(x)
    take_weights(x_left, 1)
    take_weights(x_right, 0)
    regroup(1)

    def forward_rest(n, carry):
        j = lax.rem(x + 2 * n + 1 - 3 * (n // 2), 4)

        @pl.when(n == 2)
        def _():
            take_weights(x_far, 0)
            take_weights(x_far, 1)

        arrive(part(j, 1 - c, 0), f_r.at[j, 0])
        arrive(part(j, 1 - c, 1), f_r.at[j, 1])
        forward_step(j)
        return carry

    lax.fori_loop(0, 3, forward_rest, 0)

    def pack_result(k, block):
        for xx in range(4):
            cols = slice(192 * xx, 192 * xx + 192)
            for i2 in range(2):
                rb[k, xx, i2] = jnp.concatenate(
                    [block[128 * i2 : 128 * i2 + 64, cols], block[128 * i2 + 64 : 128 * i2 + 128, cols]], axis=1
                ).reshape(4, 16, 384)

    def result_copy(k, n):
        yy, xx, dev = yx_peer(n)
        return remote(rb.at[k, xx, :, yy], t1.at[k, x, y], p_s.at[k, xx, yy], p_r.at[k, x, y], dev)

    def own_result(k):
        return pltpu.make_async_copy(rb.at[k, x, :, y], t1.at[k, x, y], l_s.at[6 + k])

    def send_result(k):
        each(1, 16, lambda n: result_copy(k, n).start())
        own_result(k).start()

    def place_copy(k, g, n):
        s, dev = zc_peer(n)
        return remote(t2.at[k, g, s], ot.at[k, me_zc, g], q_s.at[k, g, s], q_r.at[k, g, me_zc], dev)

    def own_place(k, g):
        return pltpu.make_async_copy(t2.at[k, g, me_zc], ot.at[k, me_zc, g], l_s.at[10 + 2 * k + g])

    def relay(k):
        def got(n):
            yy, xx, _ = yx_peer(n)
            arrive(t1.at[k, xx, yy], p_r.at[k, xx, yy])

        each(1, 16, got)
        own_result(k).wait()
        for g in range(2):
            t2[k, g] = dot(turn, t1[k, 2 * g : 2 * g + 2].reshape(256, 384)).astype(BF).reshape(16, 16, 384)
            each(1, 16, lambda n: place_copy(k, g, n).start())
            own_place(k, g).start()

    def placed(k, out):
        for g in range(2):
            own_place(k, g).wait()
            each(1, 16, lambda n: arrive(ot.at[k, lax.rem(me_zc + n, 16), g], q_r.at[k, g, lax.rem(me_zc + n, 16)]))
        unpair = unpair_matrix()
        for b in range(4):
            rows = ot[k, 4 * b : 4 * b + 4].reshape(128, 384)
            both = jnp.concatenate([rows[:, 0:192], rows[:, 192:384]], axis=0)
            out[:, 256 * b : 256 * b + 256] = dot_tn(both, unpair).astype(BF)

    pack_result(0, (r2[0].reshape(256, D).astype(F32) + br[...]).astype(BF))
    send_result(0)

    grouped(1)
    ctt[...] = dot_nt(order, r2[1].reshape(256, D)).astype(BF)

    def core_copy(jj):
        return remote(gb.at[jj, 1 - c], gc.at[jj], c_s.at[jj], c_r.at[jj], core_peer)

    def finish_core(jj):
        arrive(gc.at[jj], c_r.at[jj])
        hb[jj] = (gb[jj, c].astype(F32) + gc[jj].astype(F32)).astype(BF)

    left_cols, right_cols = pl.ds(0, 384), pl.ds(384, 384)

    def target(jj):
        return lax.rem(x + jj + 1, 4)

    def share_x(jj):
        return remote(hb.at[jj, :, left_cols], gx.at[x], x_s.at[jj], x_r.at[x], (m, target(jj)))

    def share_y(jj, n):
        yy, dev = y_peer(n)
        return remote(
            hb.at[jj, pl.ds(yy * 96, 96), right_cols], gy1.at[jj, y], y1_s.at[jj, yy], y1_r.at[jj, y], dev
        )

    def start_shares(jj):
        for n in (1, 3, 2):
            share_y(jj, n).start()

    def backward_step(jj, carry):
        j = target(jj)
        mc = dot_nt(r2[1].reshape(256, D), wb[j, 576:768, :])
        mc = jnp.where(kept[:, 0:1] > 0, mc, 0.0).astype(BF)
        q, kk, v = qkv[j, 0], qkv[j, 1], qkv[j, 2]
        vbd = [stack_heads(v[64 * i : 64 * i + 64]) for i in range(4)]
        kbd = [stack_heads(kk[64 * i : 64 * i + 64]) for i in range(4)]
        mcs = [only(mc[pairs[i // 2]], i % 2) for i in range(4)]
        qs = [only(q[pairs[i // 2]], i % 2) for i in range(4)]
        dws = [sum(dot_nt(vbd[2 * p + e], mcs[2 * p + e]) for e in range(2)) for p in range(2)]
        wbf = [wts[j, p].astype(BF) for p in range(2)]
        dv = [pick_heads(dot(wbf[i // 2], mcs[i])) for i in range(4)]
        dscores = []
        for p in range(2):
            weight = wts[j, p].reshape(3, 64, 128)
            dw = dws[p].reshape(3, 64, 128)
            inner = jnp.sum(dw * weight, axis=1, keepdims=True)
            dscores.append((weight * (dw - inner) * 0.125).astype(BF).reshape(192, 128))
        dq = []
        for i in range(4):
            e = i % 2
            dq.append(dot_tn(dscores[i // 2], kbd[i])[64 * e : 64 * e + 64])
        dk = [pick_heads(dot(dscores[i // 2], qs[i])) for i in range(4)]
        dq, dk, dv = [jnp.concatenate(part, axis=0).astype(BF) for part in (dq, dk, dv)]
        pcm[:, 0:192] = dq
        pcm[:, 192:384] = dk
        pcm[:, 384:576] = dv
        pcm[:, 576:768] = mx[j]
        low = iota((256, 256), 1) < 64
        tail = pcm[:, 512:768]
        tail_qkv = jnp.where(low, tail, jnp.zeros_like(tail))
        tail_mix = jnp.where(low, jnp.zeros_like(tail), tail)
        for h in range(2):
            rows = slice(384 * h, 384 * h + 384)
            gb[jj, h, :, 0:512] = dot(nt[rows, :], pcm[:, 0:512]).astype(BF)
            gb[jj, h, :, 512:768] = (dot(nt[rows, :], tail_qkv) + dot(ctt[rows, :], tail_mix)).astype(BF)
        core_copy(jj).start()
        ncot[...] += (
            dot(dq, wb[j, 0:192, :]) + dot(dk, wb[j, 192:384, :]) + dot(dv, wb[j, 384:576, :])
        )

        @pl.when(jj > 0)
        def _():
            finish_core(jj - 1)
            share_x(jj - 1).start()
            start_shares(jj - 1)

        @pl.when(jj == 1)
        def _():
            relay(0)

        return carry

    lax.fori_loop(0, 4, backward_step, 0)

    cotangent = ncot[...].astype(BF).astype(F32)
    standard = std[...]
    scaled = cotangent * gains
    mean_plain = jnp.mean(scaled, axis=-1, keepdims=True)
    mean_cross = jnp.mean(scaled * standard, axis=-1, keepdims=True)
    through = inv[:, 0:1] * (scaled - mean_plain - standard * mean_cross)
    pack_result(1, (r2[1].reshape(256, D).astype(F32) + through).astype(BF))
    send_result(1)

    gain_part = jnp.sum(cotangent * standard, axis=0, keepdims=True)
    vg[0] = jnp.concatenate(
        [gain_part[:, 192 * k : 192 * k + 192] for k in range(4)] + [jnp.zeros((4, 192), F32)], axis=0
    )
    gain_core = remote(vg.at[0], vgc, vc_s, vc_r, core_peer)
    gain_core.start()
    finish_core(3)
    start_shares(3)

    def share_x2(jj):
        return remote(hy1.at[jj], gx2.at[x], x2_s.at[jj], x2_r.at[x], (m, target(jj)))

    def sum_y1(jj):
        total = hb[jj, pl.ds(pl.multiple_of(y * 96, 16), 96), 384:768].astype(F32)
        for n in range(1, 4):
            yy = lax.rem(y + n, 4)
            arrive(gy1.at[jj, yy], y1_r.at[jj, yy])
            total = total + gy1[jj, yy].astype(F32)
        hy1[jj] = total.astype(BF)

    def sum_y1_send(jj):
        sum_y1(jj)
        share_x2(jj).start()

    each(0, 3, sum_y1_send)

    total = hb[3, :, 0:384].astype(F32)
    for n in range(1, 4):
        xx = lax.rem(x + n, 4)
        arrive(gx.at[xx], x_r.at[xx])
        total = total + gx[xx].astype(F32)
    hx[...] = total.astype(BF).reshape(4, 96, 384)

    def share_y2(n):
        yy, dev = y_peer(n)
        return remote(hx.at[yy], gy2.at[y], y2_s.at[yy], y2_r.at[y], dev)

    for n in (1, 3, 2):
        share_y2(n).start()

    arrive(vgc, vc_r)
    vg[1] = vg[0] + vgc[...]

    def gain_x(n):
        xx, dev = x_peer(n)
        return remote(vg.at[1], vgx.at[x], vx_s.at[xx], vx_r.at[x], dev)

    for n in range(1, 4):
        gain_x(n).start()

    relay(1)
    sum_y1(3)

    gain_total = vg[1]
    for n in range(1, 4):
        xx = lax.rem(x + n, 4)
        arrive(vgx.at[xx], vx_r.at[xx])
        gain_total = gain_total + vgx[xx]
    vg[2] = gain_total

    def gain_y(n):
        yy, dev = y_peer(n)
        return remote(vg.at[2], vgy.at[y], vy_s.at[yy], vy_r.at[y], dev)

    for n in range(1, 4):
        gain_y(n).start()

    left = hx[y].astype(F32)
    right = hy1[3].astype(F32)
    for n in range(1, 4):
        yy = lax.rem(y + n, 4)
        xx = lax.rem(x + n, 4)
        arrive(gy2.at[yy], y2_r.at[yy])
        arrive(gx2.at[xx], x2_r.at[xx])
        left = left + gy2[yy].astype(F32)
        right = right + gx2[xx].astype(F32)
    spread = spread_matrix()
    gzs[:, :, 0:384] = dot(spread, left.astype(BF)).astype(BF).reshape(8, 16, 384)
    gzs[:, :, 384:768] = dot(spread, right.astype(BF)).astype(BF).reshape(8, 16, 384)

    def grad_z(n):
        zz, dev = z_peer(n)
        return remote(gzs.at[zz], gz.at[z], z_s.at[zz], z_r.at[z], dev)

    for n in range(1, 8):
        grad_z(n).start()

    gain_total = vg[2]
    for n in range(1, 4):
        yy = lax.rem(y + n, 4)
        arrive(vgy.at[yy], vy_r.at[yy])
        gain_total = gain_total + vgy[yy]
    vg[3] = gain_total

    def gain_z(n):
        zz, dev = z_peer(n)
        return remote(vg.at[3], vgz.at[z], vz_s.at[zz], vz_r.at[z], dev)

    for n in range(1, 8):
        gain_z(n).start()

    placed(0, o_bo)

    total = gzs[z].astype(F32)
    gain_total = vg[3]
    for n in range(1, 8):
        zz = lax.rem(z + n, 8)
        arrive(gz.at[zz], z_r.at[zz])
        arrive(vgz.at[zz], vz_r.at[zz])
        total = total + gz[zz].astype(F32)
        gain_total = gain_total + vgz[zz]
    total = total[0:12]
    for n in range(3):
        o_gq[:, n, :] = total[:, 192 * n : 192 * n + 192].astype(BF)
    o_gp[...] = total[:, 576:768].astype(BF)
    o_gg[...] = jnp.sum(jnp.where(iota((8, 192), 0) == x, gain_total, 0.0), axis=0)

    placed(1, o_gi)

    def sent(n):
        for k in range(2):
            token_copy(k, n).wait_send()
            result_copy(k, n).wait_send()
            for g in range(2):
                place_copy(k, g, n).wait_send()

    each(1, 16, sent)
    for n in range(6):
        weight_copy(n).wait_send()
    for n in range(1, 4):
        xx = lax.rem(x + n, 4)
        swap_copy(xx, 0).wait_send()
        swap_copy(xx, 1).wait_send()
        group_copy(0, n).wait_send()
        group_copy(1, n).wait_send()
        gain_x(n).wait_send()
        share_y2(n).wait_send()
        gain_y(n).wait_send()

        def sent_y(jj):
            share_y(jj, n).wait_send()

        each(0, 4, sent_y)
    each(0, 4, lambda jj: core_copy(jj).wait_send())
    each(0, 3, lambda jj: share_x(jj).wait_send())
    each(0, 3, lambda jj: share_x2(jj).wait_send())
    for n in range(1, 8):
        grad_z(n).wait_send()
        gain_z(n).wait_send()
    gain_core.wait_send()


def body(frames_in, norm_gain, w_qkv, w_out, keep_runs, out_cotangent):
    v = lambda shape, dt=BF: pltpu.VMEM(shape, dt)
    dma = pltpu.SemaphoreType.DMA
    any_spec = pl.BlockSpec(memory_space=pl.ANY)
    vmem_spec = pl.BlockSpec(memory_space=pltpu.VMEM)
    block_out, grad_in, grad_qkv, grad_proj, grad_gain = pl.pallas_call(
        kernel,
        out_shape=(
            jax.ShapeDtypeStruct((192, 1024), BF),
            jax.ShapeDtypeStruct((192, 1024), BF),
            jax.ShapeDtypeStruct((12, 3, 192), BF),
            jax.ShapeDtypeStruct((12, 192), BF),
            jax.ShapeDtypeStruct((192,), F32),
        ),
        in_specs=[any_spec, any_spec, vmem_spec, any_spec, any_spec, vmem_spec],
        out_specs=(vmem_spec,) * 5,
        scratch_shapes=[
            v((2, 16, 16, D)),
            v((2, 4, 4, 16, D)),
            v((2, 4, 4, 16, D)),
            v((4, D, D)),
            v((256, D), F32),
            v((256, 128), F32),
            v((256, D)),
            v((D, 256)),
            v((D, 256)),
            v((256, D), F32),
            v((256, D), F32),
            v((256, 128), F32),
            v((2, 64, 128), F32),
            v((4, 3, 256, 192)),
            v((4, 2, 192, 128), F32),
            v((4, 256, 192)),
            v((256, D)),
            v((4, 2, 384, D)),
            v((4, 384, D)),
            v((4, 384, D)),
            v((4, 384, 384)),
            v((4, 4, 96, 384)),
            v((4, 96, 384)),
            v((4, 96, 384)),
            v((4, 96, 384)),
            v((4, 96, 384)),
            v((8, 16, D)),
            v((8, 16, D)),
            v((2, 4, 2, 4, 16, 384)),
            v((2, 4, 4, 2, 16, 384)),
            v((2, 2, 16, 16, 384)),
            v((2, 16, 2, 16, 384)),
            v((4, 8, 192), F32),
            v((8, 192), F32),
            v((4, 8, 192), F32),
            v((4, 8, 192), F32),
            v((8, 8, 192), F32),
            dma((2, 16)), dma((2, 16)),
            dma((2, 4)), dma((2, 4)),
            dma((6,)), dma((4, 2)),
            dma((4, 2)), dma((4, 2)),
            dma((4,)), dma((4,)),
            dma((4,)), dma((4,)),
            dma((4, 4)), dma((4, 4)),
            dma((4,)), dma((4,)),
            dma((4,)), dma((4,)),
            dma((8,)), dma((8,)),
            dma((2, 4, 4)), dma((2, 4, 4)),
            dma((2, 2, 16)), dma((2, 2, 16)),
            dma(()), dma(()),
            dma((4,)), dma((4,)),
            dma((4,)), dma((4,)),
            dma((8,)), dma((8,)),
            dma((14,)),
        ],
        compiler_params=pltpu.CompilerParams(
            collective_id=0, has_side_effects=True, vmem_limit_bytes=56 << 20
        ),
        cost_estimate=pl.CostEstimate(flops=5 * 10**9, bytes_accessed=10**7, transcendentals=200000),
        name="block",
    )(
        frames_in.reshape(1024, D),
        out_cotangent.reshape(1024, D),
        norm_gain,
        w_qkv.transpose(1, 2, 0).reshape(576, D),
        w_out,
        keep_runs.transpose(1, 2, 0),
    )
    return (
        block_out.T.reshape(1, 1024, 192),
        grad_in.T.reshape(1, 1024, 192),
        grad_qkv,
        grad_proj.T,
        grad_gain,
    )


def solution(mesh):
    in_specs = (
        P("tm", None, None),
        P(),
        P(None, None, "tensor"),
        P("tensor", None),
        P(),
        P("tm", None, None),
    )
    out_specs = (
        P("tm", None, "tensor"),
        P("tm", None, "tensor"),
        P("tm", None, "tensor"),
        P("tensor", "tm"),
        P("tensor"),
    )
    return jax.shard_map(body, mesh=mesh, in_specs=in_specs, out_specs=out_specs, check_vma=False)
```

time: 132 us -> 98.7 us (0.75)
  Pallas kernels: 119 us -> 91.6 us
  local copies, waits for them, and re-layouts: 9.97 us -> 5.32 us
  other arithmetic: 1.87 us -> 0 us
    pallas_call x1, Pallas kernels: 119 us -> 91.6 us  [body(): pl.pallas_call(kernel, out_shape=(jax.ShapeDtypeStruct((192, 1024), BF),...]
    reshape x3 -> x0, local copies, waits for them, and re-layouts: 3.51 us -> none  [the longest x1 1.54 us: body(): w_all = jnp.concatenate([w_qkv.reshape(D, 576), w_out.T], axis=1)]
where the time goes in v2:
time: 98.7 us; the launch traced here: 97.6 us
  Pallas kernels  91.6 us (93%)
  local copies, waits for them, and re-layouts  5.32 us (5%)
    pallas_call x1, Pallas kernels, body(): pl.pallas_call(kernel, out_shape=(jax.ShapeDtypeStruct((192, 1024), BF),...  91.6 us
    unnamed x11, local copies, waits for them, and re-layouts  5.32 us

profile of v2, /device:TPU:2, one launch (start us, length us, event | category | flops | bytes accessed | tf_op | source)
XLA Modules:
  0.0 97.6 jit_solution(11791658173371900959)
XLA Ops:
  0.6 91.6 %block.1 = (bf16[192,1024]{1,0:T(8,128)(2,1)}, bf16[192,1024]{1,0:T(8,128)(2,1)}, bf16[12,3,192]{2,1,0:T(4,128)(2,1)}, bf16[12,192]{1,0:T(8,128)(2,1)}, f32[192]{0:T(256)}) custom-call(bf16[1024,768]{1,0:T(8,128)(2,1)} %bitcast.16, bf16[1024,768]{1,0:T(8,128)(2,1)} %bitcast.17, f32[768]{0:T(1024)} %gain.1, bf16[576,768]{1,0:T(8,128)(2,1)} %bitcast.18, ...), custom_call_target="tpu_custom_call" | custom-call | flops 5000000000 | bytes 10000000 | tf_op jit(solution)/shard_map/block/pallas_call | solution.py:599
  92.3 0.0 copy-start
  92.3 0.0 copy-start.1
  92.3 0.0 copy-start.2
  92.3 1.8 %copy.16 = bf16[1,1024,192]{1,2,0:T(8,128)(2,1)} copy(bf16[1,1024,192]{1,2,0:T(8,128)(2,1)} %bitcast.14) | data formatting | bytes 786432
  94.1 1.8 %copy.17 = bf16[1,1024,192]{1,2,0:T(8,128)(2,1)} copy(bf16[1,1024,192]{1,2,0:T(8,128)(2,1)} %bitcast.13) | data formatting | bytes 786432
  95.8 0.0 copy-done
  95.8 0.6 copy.18
  96.4 0.0 copy-done.1
  96.4 0.6 copy.19
  97.0 0.0 copy-done.2
  97.0 0.6 copy.20
Async XLA Ops:
  92.3 3.6 %copy-start = (bf16[12,3,192]{2,1,0:T(4,128)(2,1)S(1)}, bf16[12,3,192]{2,1,0:T(4,128)(2,1)}, u32[]{:S(2)}) copy-start(bf16[12,3,192]{2,1,0:T(4,128)(2,1)} %get-tuple-element.22) | copy-start | bytes 41476
  92.3 4.2 %copy-start.1 = (bf16[12,192]{1,0:T(8,128)(2,1)S(1)}, bf16[12,192]{1,0:T(8,128)(2,1)}, u32[]{:S(2)}) copy-start(bf16[12,192]{1,0:T(8,128)(2,1)} %get-tuple-element.13) | copy-start | bytes 13828
  92.3 4.8 %copy-start.2 = (f32[192]{0:T(256)S(1)}, f32[192]{0:T(256)}, u32[]{:S(2)}) copy-start(f32[192]{0:T(256)} %get-tuple-element.24) | copy-start | bytes 2308

commit v3 on v2

--- a/solution.py
+++ b/solution.py
@@ -6,6 +6,8 @@
 from jax.sharding import PartitionSpec as P
 
 MESH = pl.DeviceIdType.MESH
+EARLY = 2
+RELAY = 2
 BF = jnp.bfloat16
 F32 = jnp.float32
 D = 768
@@ -68,10 +70,10 @@
 
 def kernel(
     fr, ct, gain, wq, wo, runs,
-    o_bo, o_gi, o_gq, o_gp, o_gg,
-    r1, s2, r2, wb, std, inv, nrm, nt, ctt, ncot, br, kept, keptw, qkv, wts, mx, pcm,
+    ot, o_gr, o_gg,
+    r1, s2, r2, wb, std, inv, nrm, nt, ctt, ncot, br, kept, qkv, wts, mx, mcs, dp, pcm,
     gb, gc, hb, gx, gy1, hy1, gx2, hx, gy2, gzs, gz,
-    rb, t1, t2, ot, vg, vgc, vgx, vgy, vgz,
+    rb, t1, t2, vg, vgc, vgx, vgy, vgz,
     a_s, a_r, b_s, b_r, w_s, w_r, f_s, f_r, c_s, c_r, x_s, x_r, y1_s, y1_r, x2_s, x2_r,
     y2_s, y2_r, z_s, z_r, p_s, p_r, q_s, q_r, vc_s, vc_r, vx_s, vx_r, vy_s, vy_r, vz_s, vz_r, l_s,
 ):
@@ -82,7 +84,9 @@
     c = lax.rem(m, 2)
     me_zc = z * 2 + c
 
-    def zc_peer(k):
+    def zc_peer(n):
+        near = (n + 1) // 2
+        k = near + (1 - lax.rem(n, 2)) * (16 - 2 * near)
         s = lax.rem(me_zc + k, 16)
         return s, ((s // 2) * 8 + y * 2 + lax.rem(s, 2), x)
 
@@ -189,10 +193,6 @@
     columns = dot_nt(frame_order_matrix(), rows)
     for i in range(4):
         kept[pl.ds(64 * i, 64), :] = jnp.broadcast_to(columns[:, i : i + 1], (64, 128))
-    first_of_pair = iota((64, 128), 1) < 64
-    for p in range(2):
-        keptw[p] = jnp.where(first_of_pair, kept[128 * p : 128 * p + 64, :], kept[128 * p + 64 : 128 * p + 128, :])
-
     def group_copy(k, n):
         yy, dev = y_peer(n)
         return remote(s2.at[k, yy], r2.at[k, :, y], b_s.at[k, yy], b_r.at[k, y], dev)
@@ -237,44 +237,32 @@
 
     lane = iota((64, 192), 1)
     head_mask = [(lane >= 64 * h) & (lane < 64 * h + 64) for h in range(3)]
-    top_rows = iota((128, 192), 0) < 64
-    nothing = jnp.zeros((128, 192), BF)
+    head_ones = [jnp.where(hm, 1.0, 0.0).astype(BF) for hm in head_mask]
 
     def stack_heads(rows):
-        return jnp.concatenate([jnp.where(hm, rows, jnp.zeros_like(rows)) for hm in head_mask], axis=0)
+        return jnp.concatenate([rows * ones for ones in head_ones], axis=0)
 
     def pick_heads(rows):
         return jnp.where(head_mask[0], rows[0:64], jnp.where(head_mask[1], rows[64:128], rows[128:192]))
 
-    def only(rows, which):
-        return jnp.where(top_rows, rows, nothing) if which == 0 else jnp.where(top_rows, nothing, rows)
-
-    pairs = [slice(128 * p, 128 * p + 128) for p in range(2)]
+    spots = [slice(64 * i, 64 * i + 64) for i in range(4)]
 
     def forward_step(j):
-        q, kk, v = [dot_nt(nrm[...], wb[j, 192 * n : 192 * n + 192, :]).astype(BF) for n in range(3)]
-        qkv[j, 0], qkv[j, 1], qkv[j, 2] = q, kk, v
-        kbd = [stack_heads(kk[64 * i : 64 * i + 64]) for i in range(4)]
-        scores = [
-            sum(dot_nt(kbd[2 * p + e], only(q[pairs[p]], e)) for e in range(2)) for p in range(2)
-        ]
-        vbd = [stack_heads(v[64 * i : 64 * i + 64]) for i in range(4)]
-        weights = []
-        for p in range(2):
-            masked = jnp.where((keptw[p] > 0)[None], scores[p].reshape(3, 64, 128) * 0.125, -1000000000.0)
-            top = jnp.max(masked, axis=1, keepdims=True)
-            expo = jnp.exp(masked - top)
-            weight = (expo / jnp.sum(expo, axis=1, keepdims=True)).reshape(192, 128)
-            wts[j, p] = weight
-            weights.append(weight.astype(BF))
-        mixed = []
+        for n in range(3):
+            qkv[j, n] = dot_nt(nrm[...], wb[j, 192 * n : 192 * n + 192, :]).astype(BF)
+        keep = [kept[spot, 0:1] > 0 for spot in spots]
+        scores = [dot_nt(qkv[j, 1, spot], stack_heads(qkv[j, 0, spot])) for spot in spots]
+        rounded = []
         for i in range(4):
-            e = i % 2
-            mixed.append(dot_tn(weights[i // 2], vbd[i])[64 * e : 64 * e + 64])
-        mixed = jnp.concatenate(mixed, axis=0)
-        mixed = jnp.where(kept[:, 0:1] > 0, mixed, 0.0).astype(BF)
-        mx[j] = mixed
-        br[...] += dot(mixed, wb[j, 576:768, :])
+            masked = jnp.where(keep[i], scores[i] * 0.125, -1000000000.0)
+            expo = jnp.exp(masked - jnp.max(masked, axis=0, keepdims=True))
+            weight = expo / jnp.sum(expo, axis=0, keepdims=True)
+            wts[j, i] = weight
+            rounded.append(weight.astype(BF))
+        crossed = [dot_tn(rounded[i], qkv[j, 2, spot]) for i, spot in enumerate(spots)]
+        mixed = [jnp.where(keep[i], pick_heads(crossed[i]), 0.0) for i in range(4)]
+        mx[j] = jnp.concatenate(mixed, axis=0).astype(BF)
+        br[...] += dot(mx[j], wb[j, 576:768, :])
 
     forward_step(x)
     take_weights(x_left, 1)
@@ -334,15 +322,10 @@
             each(1, 16, lambda n: place_copy(k, g, n).start())
             own_place(k, g).start()
 
-    def placed(k, out):
+    def placed(k):
         for g in range(2):
             own_place(k, g).wait()
             each(1, 16, lambda n: arrive(ot.at[k, lax.rem(me_zc + n, 16), g], q_r.at[k, g, lax.rem(me_zc + n, 16)]))
-        unpair = unpair_matrix()
-        for b in range(4):
-            rows = ot[k, 4 * b : 4 * b + 4].reshape(128, 384)
-            both = jnp.concatenate([rows[:, 0:192], rows[:, 192:384]], axis=0)
-            out[:, 256 * b : 256 * b + 256] = dot_tn(both, unpair).astype(BF)
 
     pack_result(0, (r2[0].reshape(256, D).astype(F32) + br[...]).astype(BF))
     send_result(0)
@@ -378,30 +361,21 @@
     def backward_step(jj, carry):
         j = target(jj)
         mc = dot_nt(r2[1].reshape(256, D), wb[j, 576:768, :])
-        mc = jnp.where(kept[:, 0:1] > 0, mc, 0.0).astype(BF)
-        q, kk, v = qkv[j, 0], qkv[j, 1], qkv[j, 2]
-        vbd = [stack_heads(v[64 * i : 64 * i + 64]) for i in range(4)]
-        kbd = [stack_heads(kk[64 * i : 64 * i + 64]) for i in range(4)]
-        mcs = [only(mc[pairs[i // 2]], i % 2) for i in range(4)]
-        qs = [only(q[pairs[i // 2]], i % 2) for i in range(4)]
-        dws = [sum(dot_nt(vbd[2 * p + e], mcs[2 * p + e]) for e in range(2)) for p in range(2)]
-        wbf = [wts[j, p].astype(BF) for p in range(2)]
-        dv = [pick_heads(dot(wbf[i // 2], mcs[i])) for i in range(4)]
+        mcs[...] = jnp.where(kept[:, 0:1] > 0, mc, 0.0).astype(BF)
+        mcb = [stack_heads(mcs[spot]) for spot in spots]
+        dws = [dot_nt(qkv[j, 2, spot], mcb[i]) for i, spot in enumerate(spots)]
+        dv = [dot(wts[j, i].astype(BF), mcb[i]) for i in range(4)]
         dscores = []
-        for p in range(2):
-            weight = wts[j, p].reshape(3, 64, 128)
-            dw = dws[p].reshape(3, 64, 128)
-            inner = jnp.sum(dw * weight, axis=1, keepdims=True)
-            dscores.append((weight * (dw - inner) * 0.125).astype(BF).reshape(192, 128))
-        dq = []
         for i in range(4):
-            e = i % 2
-            dq.append(dot_tn(dscores[i // 2], kbd[i])[64 * e : 64 * e + 64])
-        dk = [pick_heads(dot(dscores[i // 2], qs[i])) for i in range(4)]
-        dq, dk, dv = [jnp.concatenate(part, axis=0).astype(BF) for part in (dq, dk, dv)]
-        pcm[:, 0:192] = dq
-        pcm[:, 192:384] = dk
-        pcm[:, 384:576] = dv
+            weight = wts[j, i]
+            inner = jnp.sum(dws[i] * weight, axis=0, keepdims=True)
+            dscores.append((weight * (dws[i] - inner) * 0.125).astype(BF))
+        dk = [dot(dscores[i], stack_heads(qkv[j, 0, spot])) for i, spot in enumerate(spots)]
+        dq = [pick_heads(dot_tn(dscores[i], qkv[j, 1, spot])) for i, spot in enumerate(spots)]
+        for n, pieces in enumerate((dq, dk, dv)):
+            dp[n] = jnp.concatenate(pieces, axis=0).astype(BF)
+        for n in range(3):
+            pcm[:, 192 * n : 192 * n + 192] = dp[n]
         pcm[:, 576:768] = mx[j]
         low = iota((256, 256), 1) < 64
         tail = pcm[:, 512:768]
@@ -413,16 +387,19 @@
             gb[jj, h, :, 512:768] = (dot(nt[rows, :], tail_qkv) + dot(ctt[rows, :], tail_mix)).astype(BF)
         core_copy(jj).start()
         ncot[...] += (
-            dot(dq, wb[j, 0:192, :]) + dot(dk, wb[j, 192:384, :]) + dot(dv, wb[j, 384:576, :])
+            dot(dp[0], wb[j, 0:192, :]) + dot(dp[1], wb[j, 192:384, :]) + dot(dp[2], wb[j, 384:576, :])
         )
 
         @pl.when(jj > 0)
         def _():
             finish_core(jj - 1)
+
+        @pl.when((jj > 0) & (jj < EARLY + 1))
+        def _():
             share_x(jj - 1).start()
             start_shares(jj - 1)
 
-        @pl.when(jj == 1)
+        @pl.when(jj == RELAY)
         def _():
             relay(0)
 
@@ -438,6 +415,9 @@
     through = inv[:, 0:1] * (scaled - mean_plain - standard * mean_cross)
     pack_result(1, (r2[1].reshape(256, D).astype(F32) + through).astype(BF))
     send_result(1)
+    for jj in range(EARLY, 3):
+        share_x(jj).start()
+        start_shares(jj)
 
     gain_part = jnp.sum(cotangent * standard, axis=0, keepdims=True)
     vg[0] = jnp.concatenate(
@@ -463,6 +443,7 @@
         sum_y1(jj)
         share_x2(jj).start()
 
+    relay(1)
     each(0, 3, sum_y1_send)
 
     total = hb[3, :, 0:384].astype(F32)
@@ -489,7 +470,6 @@
     for n in range(1, 4):
         gain_x(n).start()
 
-    relay(1)
     sum_y1(3)
 
     gain_total = vg[1]
@@ -540,7 +520,6 @@
     for n in range(1, 8):
         gain_z(n).start()
 
-    placed(0, o_bo)
 
     total = gzs[z].astype(F32)
     gain_total = vg[3]
@@ -550,13 +529,13 @@
         arrive(vgz.at[zz], vz_r.at[zz])
         total = total + gz[zz].astype(F32)
         gain_total = gain_total + vgz[zz]
-    total = total[0:12]
-    for n in range(3):
-        o_gq[:, n, :] = total[:, 192 * n : 192 * n + 192].astype(BF)
-    o_gp[...] = total[:, 576:768].astype(BF)
-    o_gg[...] = jnp.sum(jnp.where(iota((8, 192), 0) == x, gain_total, 0.0), axis=0)
-
-    placed(1, o_gi)
+    o_gr[...] = total
+    o_gg[...] = jnp.broadcast_to(
+        jnp.sum(jnp.where(iota((8, 192), 0) == x, gain_total, 0.0), axis=0, keepdims=True), (8, 192)
+    )
+
+    placed(0)
+    placed(1)
 
     def sent(n):
         for k in range(2):
@@ -591,22 +570,34 @@
     gain_core.wait_send()
 
 
+def finish(ot, gr, gg, o_bo, o_gi, o_gq, o_gp, o_gg):
+    unpair = unpair_matrix()
+    for k, out in enumerate((o_bo, o_gi)):
+        for b in range(4):
+            rows = ot[k, 4 * b : 4 * b + 4].reshape(128, 384)
+            both = jnp.concatenate([rows[:, 0:192], rows[:, 192:384]], axis=0)
+            out[:, 256 * b : 256 * b + 256] = dot_tn(both, unpair).astype(BF)
+    total = gr[0:12, :]
+    for n in range(3):
+        o_gq[:, n, :] = total[:, 192 * n : 192 * n + 192].astype(BF)
+    o_gp[...] = total[:, 576:768].astype(BF)
+    o_gg[...] = gg[0, :]
+
+
 def body(frames_in, norm_gain, w_qkv, w_out, keep_runs, out_cotangent):
     v = lambda shape, dt=BF: pltpu.VMEM(shape, dt)
     dma = pltpu.SemaphoreType.DMA
     any_spec = pl.BlockSpec(memory_space=pl.ANY)
     vmem_spec = pl.BlockSpec(memory_space=pltpu.VMEM)
-    block_out, grad_in, grad_qkv, grad_proj, grad_gain = pl.pallas_call(
+    placed, grads, gain_sum = pl.pallas_call(
         kernel,
         out_shape=(
-            jax.ShapeDtypeStruct((192, 1024), BF),
-            jax.ShapeDtypeStruct((192, 1024), BF),
-            jax.ShapeDtypeStruct((12, 3, 192), BF),
-            jax.ShapeDtypeStruct((12, 192), BF),
-            jax.ShapeDtypeStruct((192,), F32),
+            jax.ShapeDtypeStruct((2, 16, 2, 16, 384), BF),
+            jax.ShapeDtypeStruct((16, D), F32),
+            jax.ShapeDtypeStruct((8, 192), F32),
         ),
         in_specs=[any_spec, any_spec, vmem_spec, any_spec, any_spec, vmem_spec],
-        out_specs=(vmem_spec,) * 5,
+        out_specs=(any_spec, vmem_spec, vmem_spec),
         scratch_shapes=[
             v((2, 16, 16, D)),
             v((2, 4, 4, 16, D)),
@@ -620,10 +611,11 @@
             v((256, D), F32),
             v((256, D), F32),
             v((256, 128), F32),
-            v((2, 64, 128), F32),
             v((4, 3, 256, 192)),
-            v((4, 2, 192, 128), F32),
+            v((4, 4, 64, 192), F32),
             v((4, 256, 192)),
+            v((256, 192)),
+            v((3, 256, 192)),
             v((256, D)),
             v((4, 2, 384, D)),
             v((4, 384, D)),
@@ -639,7 +631,6 @@
             v((2, 4, 2, 4, 16, 384)),
             v((2, 4, 4, 2, 16, 384)),
             v((2, 2, 16, 16, 384)),
-            v((2, 16, 2, 16, 384)),
             v((4, 8, 192), F32),
             v((8, 192), F32),
             v((4, 8, 192), F32),
@@ -676,6 +667,21 @@
         w_out,
         keep_runs.transpose(1, 2, 0),
     )
+    block_out, grad_in, grad_qkv, grad_proj, grad_gain = pl.pallas_call(
+        finish,
+        out_shape=(
+            jax.ShapeDtypeStruct((192, 1024), BF),
+            jax.ShapeDtypeStruct((192, 1024), BF),
+            jax.ShapeDtypeStruct((12, 3, 192), BF),
+            jax.ShapeDtypeStruct((12, 192), BF),
+            jax.ShapeDtypeStruct((192,), F32),
+        ),
+        in_specs=[vmem_spec] * 3,
+        out_specs=(vmem_spec,) * 5,
+        compiler_params=pltpu.CompilerParams(vmem_limit_bytes=60 << 20),
+        cost_estimate=pl.CostEstimate(flops=4 * 10**8, bytes_accessed=3 * 10**6, transcendentals=0),
+        name="finish",
+    )(placed, grads, gain_sum)
     return (
         block_out.T.reshape(1, 1024, 192),
         grad_in.T.reshape(1, 1024, 192),

time: 98.7 us -> 91.2 us (0.924)
  local copies, waits for them, and re-layouts: 5.32 us -> 0 us
  Pallas kernels: 91.6 us -> 90.4 us
    unnamed x11 -> x0, local copies, waits for them, and re-layouts: 5.32 us -> none
    pallas_call x1 -> x2, Pallas kernels: 91.6 us -> 90.4 us  [the longest x1 87.8 us: body(): pl.pallas_call(kernel, out_shape=(jax.ShapeDtypeStruct((2, 16, 2, 16, 384...]
where the time goes in v3:
time: 91.2 us; the launch traced here: 91 us
  Pallas kernels  90.4 us (99%)
    pallas_call x1, Pallas kernels, body(): pl.pallas_call(kernel, out_shape=(jax.ShapeDtypeStruct((2, 16, 2, 16, 384...  87.8 us
    pallas_call x1, Pallas kernels, body(): pl.pallas_call(finish, out_shape=(jax.ShapeDtypeStruct((192, 1024), BF),...  2.62 us

profile of v3, /device:TPU:2, one launch (start us, length us, event | category | flops | bytes accessed | tf_op | source)
XLA Modules:
  0.0 91.0 jit_solution(4883610379305451480)
XLA Ops:
  0.6 87.8 %block.1 = (bf16[2,16,2,16,384]{4,3,2,1,0:T(8,128)(2,1)}, f32[16,768]{1,0:T(8,128)}, f32[8,192]{1,0:T(8,128)}) custom-call(bf16[1024,768]{1,0:T(8,128)(2,1)} %bitcast.13, bf16[1024,768]{1,0:T(8,128)(2,1)} %bitcast.14, f32[768]{0:T(1024)} %gain.1, bf16[576,768]{1,0:T(8,128)(2,1)} %bitcast.15, bf16[192,768]{1,0:T(8,128)(2,1)} %wo.1, s32[16,2,64]{2,1,0:T(2,128)} %bitcast.16), custom_call_target="tpu_custom_call" | custom-call | flops 5000000000 | bytes 10000000 | tf_op jit(solution)/shard_map/block/pallas_call | solution.py:592
  88.4 2.6 %finish.1 = (bf16[192,1024]{1,0:T(8,128)(2,1)}, bf16[192,1024]{1,0:T(8,128)(2,1)}, bf16[12,3,192]{2,1,0:T(4,128)(2,1)}, bf16[12,192]{1,0:T(8,128)(2,1)}, f32[192]{0:T(256)}) custom-call(bf16[2,16,2,16,384]{4,3,2,1,0:T(8,128)(2,1)} %get-tuple-element.13.ot, f32[16,768]{1,0:T(8,128)} %get-tuple-element.14.gr, f32[8,192]{1,0:T(8,128)} %get-tuple-element.15.gg), custom_call_target="tpu_custom_call" | custom-call | flops 400000000 | bytes 3000000 | tf_op jit(solution)/shard_map/finish/pallas_call | solution.py:670

commit v4 on v3

--- a/solution.py
+++ b/solution.py
@@ -71,7 +71,7 @@
 def kernel(
     fr, ct, gain, wq, wo, runs,
     ot, o_gr, o_gg,
-    r1, s2, r2, wb, std, inv, nrm, nt, ctt, ncot, br, kept, qkv, wts, mx, mcs, dp, pcm,
+    r1, s2, u2, u3, u4, r2, wb, std, inv, nrm, nt, ctt, ncot, br, kept, qkv, wts, mx, mcs, dp, pcm,
     gb, gc, hb, gx, gy1, hy1, gx2, hx, gy2, gzs, gz,
     rb, t1, t2, vg, vgc, vgx, vgy, vgz,
     a_s, a_r, b_s, b_r, w_s, w_r, f_s, f_r, c_s, c_r, x_s, x_r, y1_s, y1_r, x2_s, x2_r,
@@ -139,23 +139,46 @@
     for copy in own_w:
         copy.start()
 
-    def own_rows(k):
-        ref = (fr, ct)[k]
-        return pltpu.make_async_copy(
-            ref.at[pl.ds((me_zc * 4 + x) * 16, 16)], r1.at[k, me_zc], l_s.at[1 + k]
-        )
-
-    own_rows(0).start()
-    own_rows(1).start()
+    own_rows = pltpu.make_async_copy(
+        fr.at[pl.ds((me_zc * 4 + x) * 16, 16)], r1.at[0, me_zc], l_s.at[1]
+    )
+    own_rows.start()
+    own_share = pltpu.make_async_copy(ct.at[:, x], r1.at[1], l_s.at[14])
+    own_share.start()
     turn = row_transpose_matrix()
+    own_share.wait()
+    s2[1] = dot(turn, r1[1].reshape(256, D)).astype(BF).reshape(4, 4, 16, D)
     pl.semaphore_wait(barrier, 30)
 
     def token_copy(k, n):
         s, dev = zc_peer(n)
-        rows = pl.ds((s * 4 + x) * 16, 16)
-        return remote((fr, ct)[k].at[rows], r1.at[k, me_zc], a_s.at[k, s], a_r.at[k, me_zc], dev)
+        if k == 0:
+            source, landing = fr.at[pl.ds((s * 4 + x) * 16, 16)], r1.at[0, me_zc]
+        else:
+            source, landing = u3.at[s], u4.at[me_zc]
+        return remote(source, landing, a_s.at[k, s], a_r.at[k, me_zc], dev)
+
+    def group_copy(k, n):
+        yy, dev = y_peer(n)
+        landing = r2.at[0, :, y] if k == 0 else u2.at[:, y]
+        return remote(s2.at[k, yy], landing, b_s.at[k, yy], b_r.at[k, y], dev)
+
+    def own_group(k):
+        return pltpu.make_async_copy(s2.at[k, y], r2.at[0, :, y] if k == 0 else u2.at[:, y], l_s.at[4 + k])
+
+    def send_groups(k):
+        for n in (1, 3, 2):
+            group_copy(k, n).start()
+        own_group(k).start()
+
+    def grouped(k):
+        for n in (1, 3, 2):
+            yy = lax.rem(y + n, 4)
+            arrive(r2.at[0, :, yy] if k == 0 else u2.at[:, yy], b_r.at[k, yy])
+        own_group(k).wait()
 
     each(1, 16, lambda n: token_copy(0, n).start())
+    send_groups(1)
     for copy in own_w:
         copy.wait()
 
@@ -171,8 +194,6 @@
 
     for n in range(4):
         weight_copy(n).start()
-    each(1, 16, lambda n: token_copy(1, n).start())
-
     def swap_copy(xx, ab):
         return remote(part(xx, c, ab), part(xx, c, ab), f_s.at[xx, ab], f_r.at[xx, ab], core_peer)
 
@@ -193,28 +214,24 @@
     columns = dot_nt(frame_order_matrix(), rows)
     for i in range(4):
         kept[pl.ds(64 * i, 64), :] = jnp.broadcast_to(columns[:, i : i + 1], (64, 128))
-    def group_copy(k, n):
-        yy, dev = y_peer(n)
-        return remote(s2.at[k, yy], r2.at[k, :, y], b_s.at[k, yy], b_r.at[k, y], dev)
-
-    def own_group(k):
-        return pltpu.make_async_copy(s2.at[k, y], r2.at[k, :, y], l_s.at[4 + k])
-
-    def regroup(k):
-        each(1, 16, lambda n: arrive(r1.at[k, lax.rem(me_zc + n, 16)], a_r.at[k, lax.rem(me_zc + n, 16)]))
-        own_rows(k).wait()
-        s2[k] = dot(turn, r1[k].reshape(256, D)).astype(BF).reshape(4, 4, 16, D)
-        for n in (1, 3, 2):
-            group_copy(k, n).start()
-        own_group(k).start()
-
-    def grouped(k):
-        for n in (1, 3, 2):
-            yy = lax.rem(y + n, 4)
-            arrive(r2.at[k, :, yy], b_r.at[k, yy])
-        own_group(k).wait()
-
-    regroup(0)
+    own_column = pltpu.make_async_copy(u3.at[me_zc], u4.at[me_zc], l_s.at[2])
+
+    def pass_cotangent():
+        grouped(1)
+        u3[...] = dot(turn, u2[...].reshape(256, D)).astype(BF).reshape(16, 16, D)
+        each(1, 16, lambda n: token_copy(1, n).start())
+        own_column.start()
+
+    def take_cotangent():
+        each(1, 16, lambda n: arrive(u4.at[lax.rem(me_zc + n, 16)], a_r.at[1, lax.rem(me_zc + n, 16)]))
+        own_column.wait()
+        r2[1] = dot(turn, u4[...].reshape(256, D)).astype(BF).reshape(4, 4, 16, D)
+
+    pass_cotangent()
+    each(1, 16, lambda n: arrive(r1.at[0, lax.rem(me_zc + n, 16)], a_r.at[0, lax.rem(me_zc + n, 16)]))
+    own_rows.wait()
+    s2[0] = dot(turn, r1[0].reshape(256, D)).astype(BF).reshape(4, 4, 16, D)
+    send_groups(0)
     take_weights(x_left, 0)
     weight_copy(4).start()
     take_weights(x_right, 1)
@@ -267,7 +284,6 @@
     forward_step(x)
     take_weights(x_left, 1)
     take_weights(x_right, 0)
-    regroup(1)
 
     def forward_rest(n, carry):
         j = lax.rem(x + 2 * n + 1 - 3 * (n // 2), 4)
@@ -330,7 +346,7 @@
     pack_result(0, (r2[0].reshape(256, D).astype(F32) + br[...]).astype(BF))
     send_result(0)
 
-    grouped(1)
+    take_cotangent()
     ctt[...] = dot_nt(order, r2[1].reshape(256, D)).astype(BF)
 
     def core_copy(jj):
@@ -601,6 +617,9 @@
         scratch_shapes=[
             v((2, 16, 16, D)),
             v((2, 4, 4, 16, D)),
+            v((4, 4, 16, D)),
+            v((16, 16, D)),
+            v((16, 16, D)),
             v((2, 4, 4, 16, D)),
             v((4, D, D)),
             v((256, D), F32),
@@ -652,7 +671,7 @@
             dma((4,)), dma((4,)),
             dma((4,)), dma((4,)),
             dma((8,)), dma((8,)),
-            dma((14,)),
+            dma((15,)),
         ],
         compiler_params=pltpu.CompilerParams(
             collective_id=0, has_side_effects=True, vmem_limit_bytes=56 << 20
@@ -661,7 +680,7 @@
         name="block",
     )(
         frames_in.reshape(1024, D),
-        out_cotangent.reshape(1024, D),
+        out_cotangent.reshape(16, 4, 16, D),
         norm_gain,
         w_qkv.transpose(1, 2, 0).reshape(576, D),
         w_out,

time: 91.2 us -> 91 us (level)
  no operation moved by 1% of the time
where the time goes in v4:
time: 91 us; the launch traced here: 90.8 us
  Pallas kernels  90.2 us (99%)
    pallas_call x1, Pallas kernels, body(): pl.pallas_call(kernel, out_shape=(jax.ShapeDtypeStruct((2, 16, 2, 16, 384...  87.5 us
    pallas_call x1, Pallas kernels, body(): pl.pallas_call(finish, out_shape=(jax.ShapeDtypeStruct((192, 1024), BF),...  2.62 us

profile of v4, /device:TPU:2, one launch (start us, length us, event | category | flops | bytes accessed | tf_op | source)
XLA Modules:
  0.0 90.8 jit_solution(8444842754258166497)
XLA Ops:
  0.6 87.5 %block.1 = (bf16[2,16,2,16,384]{4,3,2,1,0:T(8,128)(2,1)}, f32[16,768]{1,0:T(8,128)}, f32[8,192]{1,0:T(8,128)}) custom-call(bf16[1024,768]{1,0:T(8,128)(2,1)} %bitcast.13, bf16[16,4,16,768]{3,2,1,0:T(8,128)(2,1)} %bitcast.14, f32[768]{0:T(1024)} %gain.1, bf16[576,768]{1,0:T(8,128)(2,1)} %bitcast.15, bf16[192,768]{1,0:T(8,128)(2,1)} %wo.1, s32[16,2,64]{2,1,0:T(2,128)} %bitcast.16), custom_call_target="tpu_custom_call" | custom-call | flops 5000000000 | bytes 10000000 | tf_op jit(solution)/shard_map/block/pallas_call | solution.py:608
  88.2 2.6 %finish.1 = (bf16[192,1024]{1,0:T(8,128)(2,1)}, bf16[192,1024]{1,0:T(8,128)(2,1)}, bf16[12,3,192]{2,1,0:T(4,128)(2,1)}, bf16[12,192]{1,0:T(8,128)(2,1)}, f32[192]{0:T(256)}) custom-call(bf16[2,16,2,16,384]{4,3,2,1,0:T(8,128)(2,1)} %get-tuple-element.13.ot, f32[16,768]{1,0:T(8,128)} %get-tuple-element.14.gr, f32[8,192]{1,0:T(8,128)} %get-tuple-element.15.gg), custom_call_target="tpu_custom_call" | custom-call | flops 400000000 | bytes 3000000 | tf_op jit(solution)/shard_map/finish/pallas_call | solution.py:689

commit v5 on v4

--- a/solution.py
+++ b/solution.py
@@ -237,6 +237,8 @@
     take_weights(x_right, 1)
     weight_copy(5).start()
     grouped(0)
+    take_weights(x_left, 1)
+    take_weights(x_right, 0)
 
     tokens = r2[0].reshape(256, D).astype(F32)
     centre = jnp.mean(tokens, axis=-1, keepdims=True)
@@ -282,13 +284,11 @@
         br[...] += dot(mx[j], wb[j, 576:768, :])
 
     forward_step(x)
-    take_weights(x_left, 1)
-    take_weights(x_right, 0)
 
     def forward_rest(n, carry):
         j = lax.rem(x + 2 * n + 1 - 3 * (n // 2), 4)
 
-        @pl.when(n == 2)
+        @pl.when(n == 1)
         def _():
             take_weights(x_far, 0)
             take_weights(x_far, 1)

time: 91 us -> 89.6 us (0.985); the launches traced: 90.8 us -> 87.9 us
  Pallas kernels: 90.2 us -> 87.2 us
    pallas_call x1, Pallas kernels: 87.5 us -> 84.6 us  [body(): pl.pallas_call(kernel, out_shape=(jax.ShapeDtypeStruct((2, 16, 2, 16, 384...]
where the time goes in v5:
time: 89.6 us; the launch traced here: 87.9 us
  Pallas kernels  87.2 us (97%)
    pallas_call x1, Pallas kernels, body(): pl.pallas_call(kernel, out_shape=(jax.ShapeDtypeStruct((2, 16, 2, 16, 384...  84.6 us
    pallas_call x1, Pallas kernels, body(): pl.pallas_call(finish, out_shape=(jax.ShapeDtypeStruct((192, 1024), BF),...  2.62 us

profile of v5, /device:TPU:2, one launch (start us, length us, event | category | flops | bytes accessed | tf_op | source)
XLA Modules:
  0.0 87.9 jit_solution(13569122503631556949)
XLA Ops:
  0.6 84.6 %block.1 = (bf16[2,16,2,16,384]{4,3,2,1,0:T(8,128)(2,1)}, f32[16,768]{1,0:T(8,128)}, f32[8,192]{1,0:T(8,128)}) custom-call(bf16[1024,768]{1,0:T(8,128)(2,1)} %bitcast.13, bf16[16,4,16,768]{3,2,1,0:T(8,128)(2,1)} %bitcast.14, f32[768]{0:T(1024)} %gain.1, bf16[576,768]{1,0:T(8,128)(2,1)} %bitcast.15, bf16[192,768]{1,0:T(8,128)(2,1)} %wo.1, s32[16,2,64]{2,1,0:T(2,128)} %bitcast.16), custom_call_target="tpu_custom_call" | custom-call | flops 5000000000 | bytes 10000000 | tf_op jit(solution)/shard_map/block/pallas_call | solution.py:608
  85.2 2.6 %finish.1 = (bf16[192,1024]{1,0:T(8,128)(2,1)}, bf16[192,1024]{1,0:T(8,128)(2,1)}, bf16[12,3,192]{2,1,0:T(4,128)(2,1)}, bf16[12,192]{1,0:T(8,128)(2,1)}, f32[192]{0:T(256)}) custom-call(bf16[2,16,2,16,384]{4,3,2,1,0:T(8,128)(2,1)} %get-tuple-element.13.ot, f32[16,768]{1,0:T(8,128)} %get-tuple-element.14.gr, f32[8,192]{1,0:T(8,128)} %get-tuple-element.15.gg), custom_call_target="tpu_custom_call" | custom-call | flops 400000000 | bytes 3000000 | tf_op jit(solution)/shard_map/finish/pallas_call | solution.py:689
